TPU v7x, 256 devices: a whole 4x4x8 slice. The times are simulated.
256 devices in a mesh: section: 2 (over y_lo), fsdp: 32 (over x, z), dp: 4 (over y_hi, core).
Axes of the slice: x: 4, y: 4 (y_hi: 2, y_lo: 2; y = y_hi * 2 + y_lo), z: 8, core: 2. Of those that a mesh axis runs over, the one named last changes fastest.
Arguments:
- activations: bfloat16 [2, 4, 4096, 3584], P('section', None, ('fsdp', 'dp')), may hold values from -6 to 6
- out_grad: bfloat16 [2, 4, 4096, 14336], P('section', None, ('fsdp', 'dp')), may hold values from -6 to 6
- blocks: bfloat16 [2, 128, 128, 128], P('section', 'fsdp'), may hold values from -0.5 to 0.5
- pattern: int32 [2, 128, 2], P('section', 'fsdp'), may hold values from 0 to 111, as said below
- order: int32 [4], replicated, may hold values from 0 to 3, each once
Outputs:
- received: bfloat16 [2, 4, 4096, 3584], P('section', None, ('fsdp', 'dp'))
- weight_grad: float32 [2, 128, 128, 128], P('section', 'fsdp')
Inputs may be any that keep to these rules, and one draw needn't show every extreme that they name: pattern[s, b, 0] < 28 and pattern[s, b, 1] < 112; no two blocks of one section share both indices; within a section the blocks stand in ascending order of (row, column). `order`: a permutation of the microbatches.
All inputs are finite; a program needn't handle non-finite values.
Results may differ from a plain program's by a relative error of at most 0.0049.
Values may be sent and summed in bfloat16 or wider, within the bound.
A program may use at most 128 MiB of HBM per device.

v0:
```python
import math

import jax
import jax.numpy as jnp
from jax import lax
from jax.sharding import PartitionSpec as P


def passed_along(block, axis, distance):
    devices = range(lax.axis_size(axis))
    route = [(i - distance, i) for i in devices if i - distance in devices]
    return lax.ppermute(block, axis, route)


def silu_slope(pre_act):
    sigmoid_val = jax.nn.sigmoid(pre_act)
    return sigmoid_val * (1.0 + pre_act * (1.0 - sigmoid_val))


def in_groups(step_fn, running, shard_blocks):
    block_count = shard_blocks.shape[0]
    group_size = math.gcd(block_count, 32)

    def one_group(number, carried):
        segment = lax.dynamic_slice_in_dim(shard_blocks, number * group_size, group_size, 0)
        return step_fn(carried, segment, number * group_size)

    return lax.fori_loop(0, block_count // group_size, one_group, running)


def local(activations, out_grad, blocks, pattern, order):
    block_size = blocks.shape[-1]
    micro_count = activations.shape[1]
    tok_rows = activations.shape[1] * activations.shape[2]
    row_count = activations.shape[3] // block_size
    col_count = out_grad.shape[3] // block_size
    features = activations[0].reshape(tok_rows, row_count, block_size)
    hidden_grad = out_grad[0].reshape(tok_rows, out_grad.shape[3])
    own_blocks = blocks[0]
    all_indices = lax.all_gather(pattern[0], "fsdp", axis=0, tiled=True)

    def forward_step(running, shard_blocks, first_block):
        indices = lax.dynamic_slice_in_dim(all_indices, first_block, shard_blocks.shape[0], 0)
        rows_in = jnp.take(features, indices[:, 0], axis=1)
        product = jnp.einsum(
            "tbk,bkn->tbn", rows_in, shard_blocks, preferred_element_type=jnp.float32
        )
        return running.at[:, indices[:, 1]].add(product)

    pre_zero = jnp.zeros((tok_rows, col_count, block_size), jnp.float32)
    pre_act = in_groups(
        forward_step, pre_zero, lax.all_gather(own_blocks, "fsdp", axis=0, tiled=True)
    )
    act_grad = (hidden_grad.astype(jnp.float32) * silu_slope(pre_act.reshape(tok_rows, -1))).astype(
        jnp.bfloat16
    )
    grad_cols = act_grad.reshape(tok_rows, col_count, block_size)

    def backward_step(running, shard_blocks, first_block):
        indices = lax.dynamic_slice_in_dim(all_indices, first_block, shard_blocks.shape[0], 0)
        cols_in = jnp.take(grad_cols, indices[:, 1], axis=1)
        product = jnp.einsum(
            "tbn,bkn->tbk", cols_in, shard_blocks, preferred_element_type=jnp.float32
        )
        return running.at[:, indices[:, 0]].add(product)

    back_zero = jnp.zeros((tok_rows, row_count, block_size), jnp.float32)
    input_grad = in_groups(
        backward_step, back_zero, lax.all_gather(own_blocks, "fsdp", axis=0, tiled=True)
    )
    input_grad = input_grad.astype(jnp.bfloat16).reshape(
        micro_count, activations.shape[2], activations.shape[3]
    )
    ordered = jnp.take(input_grad, order, axis=0)
    received = passed_along(ordered, "section", -1)
    indices = all_indices
    rows_in = jnp.take(features, indices[:, 0], axis=1)
    cols_in = jnp.take(grad_cols, indices[:, 1], axis=1)
    owned_grads = lax.psum_scatter(
        jnp.einsum("tbk,tbn->bkn", rows_in, cols_in, preferred_element_type=jnp.float32),
        "fsdp",
        scatter_dimension=0,
        tiled=True,
    )
    summed = lax.psum(owned_grads, "dp")
    grad_scale = 1.0 / math.sqrt(tok_rows * lax.axis_size("fsdp") * lax.axis_size("dp"))
    return (received[None], (summed * grad_scale)[None])


def solution(mesh):
    in_specs = (
        P("section", None, ("fsdp", "dp"), None),
        P("section", None, ("fsdp", "dp"), None),
        P("section", "fsdp", None, None),
        P("section", "fsdp", None),
        P(),
    )
    out_specs = (P("section", None, ("fsdp", "dp"), None), P("section", "fsdp", None, None))
    return jax.shard_map(local, mesh=mesh, in_specs=in_specs, out_specs=out_specs, check_vma=False)
```

profile of v0, /device:TPU:9, one launch (start us, length us, event | category | flops | bytes accessed | tf_op | source)
XLA Modules:
  0.0 443.3 jit_solution(14893785248069533942)
XLA Ops:
  7.2 0.0 all-gather.4.cloned.1.call-start
  7.2 0.7 all-gather.4.cloned.1.call-update
  7.9 0.0 reduce-scatter.2.cloned.1.call-start
  7.9 0.8 copy.31
  8.7 40.6 %all-gather = s32[1,128,2]{2,0,1:T(1,128)S(1)} all-gather(s32[1,4,2]{2,0,1:T(1,128)S(1)} %copy.31), channel_id=2, replica_groups=mesh['section'=2,'fsdp'=32,'dp'=4] {'fsdp'}, dimensions={1}, use_global_device_ids=true | all-gather | bytes 1056 | tf_op jit(solution)/shard_map/all_gather | solution.py:40
  49.3 0.1 copy.36
  49.3 1.6 reshape_squeeze.4
  51.0 0.4 copy.34
  51.4 5.9 %copy.41 = f32[16,8,112,128]{3,2,1,0:T(8,128)} copy(bf16[16,8,112,128]{3,1,2,0:T(8,128)(2,1)} %bitcast.51) | data formatting | bytes 11010048
  57.2 0.2 fusion.29
  57.4 3.1 gather_fusion.3
  60.5 0.2 and_reduce_fusion.1
  60.7 31.9 %all-gather.4.cloned.1.call-done = bf16[1,128,128,128]{3,2,0,1:T(8,128)(2,1)} async-done(((bf16[1,4,128,128]{3,2,0,1:T(8,128)(2,1)}), bf16[1,128,128,128]{3,2,0,1:T(8,128)(2,1)}) %all-gather.4.cloned.1.call-update) | async-done | bytes 4194320 | tf_op jit(solution)/shard_map/all_gather | solution.py:69
  92.6 3.9 broadcast_in_dim.90
  96.5 40.3 %while.26 = (s32[]{:T(128)}, f32[128,112,128]{2,0,1:T(8,128)}, s32[128,2]{0,1:T(2,128)S(1)}, bf16[128,128,128]{2,1,0:T(8,128)(2,1)}, bf16[128,28,128]{2,0,1:T(8,...) while((s32[]{:T(128)}, f32[128,112,128]{2,0,1:T(8,128)}, s32[128,2]{0,1:T(2,128)S(1)}, ...), condition=%wide.region_2.3_spmd, body=%wide.region_0.2_spmd.sunk | while | flops 135267712 | bytes 12588755 | solution.py:28
  96.5 0.1 constant_dynamic-slice_fusion.4
  96.6 1.7 gather_fusion
  98.3 2.0 fusion.43
  100.3 6.2 %scatter_fusion = f32[128,112,128]{2,0,1:T(8,128)} fusion(f32[128,112,128]{2,0,1:T(8,128)} %get-tuple-element.332, s32[32]{0:T(128)S(1)} %get-tuple-element.313, f32[32,128,128]{2,1,0:T(8,128)S(1)} %fusion.43), kind=kCustom, calls=%fused_computation.5.clone.1 | custom fusion | flops 524288 | bytes 6291584 | tf_op jit(solution)/shard_map/while/body/eval_jaxpr/scatter-add | solution.py:48
  106.6 0.1 constant_dynamic-slice_fusion.4
  106.7 1.7 gather_fusion
  108.4 2.0 fusion.43
  110.4 6.3 %scatter_fusion = f32[128,112,128]{2,0,1:T(8,128)} fusion(f32[128,112,128]{2,0,1:T(8,128)} %get-tuple-element.332, s32[32]{0:T(128)S(1)} %get-tuple-element.313, f32[32,128,128]{2,1,0:T(8,128)S(1)} %fusion.43), kind=kCustom, calls=%fused_computation.5.clone.1 | custom fusion | flops 524288 | bytes 6291584 | tf_op jit(solution)/shard_map/while/body/eval_jaxpr/scatter-add | solution.py:48
  116.7 0.1 constant_dynamic-slice_fusion.4
  116.8 1.7 gather_fusion
  118.4 2.0 fusion.43
  120.5 6.2 %scatter_fusion = f32[128,112,128]{2,0,1:T(8,128)} fusion(f32[128,112,128]{2,0,1:T(8,128)} %get-tuple-element.332, s32[32]{0:T(128)S(1)} %get-tuple-element.313, f32[32,128,128]{2,1,0:T(8,128)S(1)} %fusion.43), kind=kCustom, calls=%fused_computation.5.clone.1 | custom fusion | flops 524288 | bytes 6291584 | tf_op jit(solution)/shard_map/while/body/eval_jaxpr/scatter-add | solution.py:48
  126.7 0.1 constant_dynamic-slice_fusion.4
  126.8 1.7 gather_fusion
  128.5 2.0 fusion.43
  130.5 6.3 %scatter_fusion = f32[128,112,128]{2,0,1:T(8,128)} fusion(f32[128,112,128]{2,0,1:T(8,128)} %get-tuple-element.332, s32[32]{0:T(128)S(1)} %get-tuple-element.313, f32[32,128,128]{2,1,0:T(8,128)S(1)} %fusion.43), kind=kCustom, calls=%fused_computation.5.clone.1 | custom fusion | flops 524288 | bytes 6291584 | tf_op jit(solution)/shard_map/while/body/eval_jaxpr/scatter-add | solution.py:48
  136.8 8.5 %fusion.20 = bf16[128,112,128]{2,0,1:T(8,128)(2,1)} fusion(f32[128,112,128]{2,1,0:T(8,128)} %bitcast.49, f32[128,112,128]{2,0,1:T(8,128)} %get-tuple-element.190), kind=kLoop, calls=%fused_computation.38 | loop fusion | flops 16515072 | bytes 18350080 | tf_op jit(solution)/shard_map/convert_element_type | solution.py:54
  145.3 5.1 %gather_fusion.4 = bf16[128,128,128]{2,1,0:T(8,128)(2,1)} fusion(bf16[128,112,128]{2,0,1:T(8,128)(2,1)} %fusion.20, s32[1024]{0:T(1024)S(1)} %get-tuple-element.250), kind=kCustom, calls=%fused_computation.4 | custom fusion | bytes 8389120 | tf_op jit(solution)/shard_map/jit(_take)/gather | solution.py:78
  150.4 8.5 %fusion.21 = f32[128,128,128]{2,1,0:T(8,128)} fusion(bf16[128,128,128]{2,1,0:T(8,128)(2,1)} %gather_fusion.4, bf16[128,128,128]{2,1,0:T(8,128)(2,1)} %gather_fusion.3, pred[128]{0:T(512)(128)(4,1)S(1)} %get-tuple-element.223, pred[128]{0:T(512)(128)(4,1)S(1)} %get-tuple-element.222), kind=kOutput, calls=%fused_computation.39 | convolution fusion | flops 541065216 | bytes 16777472 | tf_op jit(solution)/shard_map/tbk,tbn->bkn/dot_general | solution.py:80
  159.0 0.2 all-reduce.2.cloned.1.call-start
  159.2 0.4 copy-done
  159.6 1.5 broadcast_in_dim.89
  161.1 45.6 %while.27 = (s32[]{:T(128)}, f32[128,28,128]{2,0,1:T(8,128)}, s32[128,2]{0,1:T(2,128)S(1)}, bf16[128,128,128]{2,1,0:T(8,128)(2,1)}, bf16[128,112,128]{2,0,1:T(8,...) while((s32[]{:T(128)}, f32[128,28,128]{2,0,1:T(8,128)}, s32[128,2]{0,1:T(2,128)S(1)}, ...), condition=%wide.region_5.6_spmd, body=%wide.region_3.5_spmd.sunk | while | flops 135267712 | bytes 12588755 | solution.py:28
  161.1 0.1 constant_dynamic-slice_fusion.5
  161.2 2.8 gather_fusion.1
  164.0 2.1 fusion.47
  166.1 6.2 %scatter_fusion.1 = f32[128,28,128]{2,0,1:T(8,128)} fusion(f32[128,28,128]{2,0,1:T(8,128)} %get-tuple-element.359, s32[32]{0:T(128)S(1)} %get-tuple-element.320, f32[32,128,128]{2,1,0:T(8,128)S(1)} %fusion.47), kind=kCustom, calls=%fused_computation.6.clone.1 | custom fusion | flops 524288 | bytes 6291584 | tf_op jit(solution)/shard_map/while/body/eval_jaxpr/scatter-add | solution.py:65
  172.3 0.1 constant_dynamic-slice_fusion.5
  172.4 2.8 gather_fusion.1
  175.2 2.1 fusion.47
  177.3 6.5 %scatter_fusion.1 = f32[128,28,128]{2,0,1:T(8,128)} fusion(f32[128,28,128]{2,0,1:T(8,128)} %get-tuple-element.359, s32[32]{0:T(128)S(1)} %get-tuple-element.320, f32[32,128,128]{2,1,0:T(8,128)S(1)} %fusion.47), kind=kCustom, calls=%fused_computation.6.clone.1 | custom fusion | flops 524288 | bytes 6291584 | tf_op jit(solution)/shard_map/while/body/eval_jaxpr/scatter-add | solution.py:65
  183.9 0.1 constant_dynamic-slice_fusion.5
  184.0 2.8 gather_fusion.1
  186.8 2.1 fusion.47
  188.9 6.2 %scatter_fusion.1 = f32[128,28,128]{2,0,1:T(8,128)} fusion(f32[128,28,128]{2,0,1:T(8,128)} %get-tuple-element.359, s32[32]{0:T(128)S(1)} %get-tuple-element.320, f32[32,128,128]{2,1,0:T(8,128)S(1)} %fusion.47), kind=kCustom, calls=%fused_computation.6.clone.1 | custom fusion | flops 524288 | bytes 6291584 | tf_op jit(solution)/shard_map/while/body/eval_jaxpr/scatter-add | solution.py:65
  195.1 0.1 constant_dynamic-slice_fusion.5
  195.2 2.9 gather_fusion.1
  198.1 2.1 fusion.47
  200.2 6.4 %scatter_fusion.1 = f32[128,28,128]{2,0,1:T(8,128)} fusion(f32[128,28,128]{2,0,1:T(8,128)} %get-tuple-element.359, s32[32]{0:T(128)S(1)} %get-tuple-element.320, f32[32,128,128]{2,1,0:T(8,128)S(1)} %fusion.47), kind=kCustom, calls=%fused_computation.6.clone.1 | custom fusion | flops 524288 | bytes 6291584 | tf_op jit(solution)/shard_map/while/body/eval_jaxpr/scatter-add | solution.py:65
  206.6 1.6 convert_element_type.17
  208.3 0.6 copy.37
  208.9 0.5 reshape.37
  209.4 0.6 gather_fusion.2
  210.0 0.2 broadcast_select_fusion
  210.2 1.7 collective-permute-start
  211.9 171.9 %reduce-scatter.2.cloned.1.call-done = f32[4,128,128]{2,1,0:T(8,128)} async-done(((f32[128,128,128]{2,1,0:T(8,128)}), f32[4,128,128]{2,1,0:T(8,128)}) %reduce-scatter.2.cloned.1.call-update) | async-done | bytes 262160 | tf_op jit(solution)/shard_map/reduce_scatter | solution.py:79
  383.8 50.4 %all-reduce.2.cloned.1.call-done = f32[4,128,128]{2,1,0:T(8,128)} async-done(((f32[4,128,128]{2,1,0:T(8,128)}), f32[4,128,128]{2,1,0:T(8,128)}) %all-reduce.2.cloned.1.call-update) | async-done | bytes 262160 | tf_op jit(solution)/shard_map/psum | solution.py:85
  434.2 1.7 multiply_bitcast_fusion
  435.8 0.9 copy.61
  (32 shorter events, 0.3 us)
Async XLA Ops:
  7.2 85.4 %all-gather.4.cloned.1.call-start = ((), (), s32[]{:S(2)}) async-start(), calls=%async_computation.3 | async-start | bytes 4325376 | tf_op jit(solution)/shard_map/all_gather | solution.py:69
  7.9 375.9 %reduce-scatter.2.cloned.1.call-start = ((), (), s32[]{:S(2)}) async-start(), calls=%async_computation.1 | async-start | bytes 8650752 | tf_op jit(solution)/shard_map/reduce_scatter | solution.py:79
  158.9 0.7 copy-start
  159.0 275.2 %all-reduce.2.cloned.1.call-start = ((), (), s32[]{:S(2)}) async-start(), calls=%async_computation.2 | async-start | bytes 524288 | tf_op jit(solution)/shard_map/psum | solution.py:85
  210.2 173.6 %collective-permute-start = (bf16[4,32,3584]{2,1,0:T(8,128)(2,1)S(1)}, bf16[4,32,3584]{2,1,0:T(8,128)(2,1)S(1)}, u32[]{:S(2)}, u32[]{:S(2)}) collective-permute-start(bf16[4,32,3584]{2,1,0:T(8,128)(2,1)S(1)} %broadcast_select_fusion), channel_id=1, source_target_pairs={{128,0},{129,1},{130,2},{131,3},{132,4},{133,5},{134,6},{135,7},{1... | collective-permute-start | bytes 2752520 | tf_op jit(solution)/shard_map/ppermute | solution.py:12
Sparse Core Ops, SparseCore 0:
  10.6 81.9 all-gather.3
  159.1 224.6 reduce-scatter.1
  386.6 47.5 all-reduce.1
where the time goes:
time: 447 us; the launch traced here: 443 us
  waiting for transfers between devices  255 us (57%)
  other arithmetic  63 us (14%)
  local copies, waits for them, and re-layouts  43.9 us (10%)
  blocking collectives  40.6 us (9%)
  matrix products  25.1 us (6%)
  between operations  13.8 us (3%)
    reduce_scatter x1, waiting for transfers between devices, local(): lax.psum_scatter(jnp.einsum('tbk,tbn->bkn', rows_in, cols_in, preferred_e...  172 us
    psum x1, waiting for transfers between devices, local(): summed = lax.psum(owned_grads, 'dp')  50.4 us
    all_gather x1, blocking collectives, local(): all_indices = lax.all_gather(pattern[0], 'fsdp', axis=0, tiled=True)  40.6 us
    all_gather x1, waiting for transfers between devices, local(): lax.all_gather(own_blocks, 'fsdp', axis=0, tiled=True)  31.9 us
    scatter-add x4, other arithmetic, backward_step(): return running.at[:, indices[:, 0]].add(product)  25.4 us
    scatter-add x4, other arithmetic, forward_step(): return running.at[:, indices[:, 1]].add(product)  25.1 us
    gather x4, local copies, waits for them, and re-layouts, backward_step(): cols_in = jnp.take(grad_cols, indices[:, 1], axis=1)  11.2 us
  transfers between devices with their start and end apart: 4, of which 3 were waited for; matrix products, arithmetic and copies ran while one was open for 14% of the time, Pallas kernels for 0%

commit v1 on v0

v1 whole, which is shorter than its diff:
```python
import heapq
import itertools

import jax
import jax.numpy as jnp
from jax import lax
from jax.experimental import pallas as pl
from jax.experimental.pallas import tpu as pltpu
from jax.sharding import PartitionSpec as P

MESH = pl.DeviceIdType.MESH
X, Z = 4, 8
Q = 4
BS = 128
NBLK = X * Z * Q
F32, BF16, I32 = jnp.float32, jnp.bfloat16, jnp.int32


class Place:
    def __init__(self):
        fsdp, dp = lax.axis_index("fsdp"), lax.axis_index("dp")
        self.x, self.z = fsdp // Z, lax.rem(fsdp, Z)
        self.core = lax.rem(dp, 2)
        self.section = lax.axis_index("section")
        self.sibling = {"dp": dp + 1 - 2 * self.core}
        self.twin = {"dp": lax.rem(dp + 2, 4)}
        self.other_section = {"section": 1 - self.section}

    def at(self, dx, dz):
        return lax.rem(self.x + dx + X, X), lax.rem(self.z + dz + Z, Z)

    def device(self, dx, dz):
        x, z = self.at(dx, dz)
        return {"fsdp": x * Z + z}


class Copies:
    def __init__(self, send, recv):
        self.send, self.recv, self.used, self.made = send, recv, 0, []

    def start(self, src, dst, device):
        n = self.used
        self.used += 1
        copy = pltpu.make_async_remote_copy(
            src_ref=src, dst_ref=dst, send_sem=self.send.at[n], recv_sem=self.recv.at[n],
            device_id=device, device_id_type=MESH)
        copy.start()
        self.made.append(copy)
        return copy

    def finish(self):
        for copy in self.made:
            copy.wait_send()


def meet(devices):
    barrier = pltpu.get_barrier_semaphore()
    for device in devices:
        pl.semaphore_signal(barrier, inc=1, device_id=device, device_id_type=MESH)
    pl.semaphore_wait(barrier, len(devices))


DIRS = {"x+": (1, 0), "x-": (-1, 0), "z+": (0, 1), "z-": (0, -1)}


def onward(kind, dx, dz):
    out = []
    if kind == 0:
        if dx == 0:
            if -3 <= dz <= 0:
                out.append("z+")
            if 0 <= dz <= 2:
                out.append("z-")
            out += ["x+", "x-"]
        elif dx == -1 and dz in (0, -1, -2, -3):
            out.append("x+")
        elif dx == 1 and dz in (-4, 1, 2, 3):
            out.append("x-")
        return out
    if dz == 0:
        out += ["z+", "z-"]
        if dx == 0:
            out += ["x+", "x-"]
        elif dx == -1:
            out.append("x+")
        return out
    if dz < 0 and (dz > -3 or (dz == -3 and dx in (0, -2))):
        out.append("z+")
    if dz > 0 and (dz < 3 or (dz == 3 and dx in (-1, 1))):
        out.append("z-")
    return out


def gather_order(first=0.7, hop=1.0):
    free = dict.fromkeys(DIRS, 0.0)
    tick = itertools.count()
    due = [(0.0, next(tick), 0, 0, 0, None), (0.0, next(tick), 1, 0, 0, None)]
    order = []
    while due:
        now, _, kind, dx, dz, came = heapq.heappop(due)
        order.append((kind, dx, dz, came))
        for way in onward(kind, dx, dz):
            begin = max(free[way], now)
            free[way] = begin + first
            ddx, ddz = DIRS[way]
            heapq.heappush(due, (begin + first + hop, next(tick), kind, dx - ddx, dz - ddz, way))
    return order


GATHER = gather_order()
N_GATHER = 62 + 62 + 10


def gather_kernel(blocks_ref, pat_ref, w_ref, p_ref, send, recv):
    me = Place()
    line_z = [me.device(0, k) for k in range(1, Z)]
    line_x = [me.device(k, 0) for k in range(1, X)]
    meet(line_z + line_x + [me.sibling])
    copies = Copies(send, recv)

    x, z = me.at(0, 0)
    w_ref[x, z] = blocks_ref[...]
    p_ref[x, z] = pat_ref[...]
    pats = [copies.start(pat_ref, p_ref.at[x, z], d) for d in line_z]

    coming, shared = {}, []
    for kind, dx, dz, came in GATHER:
        bx, bz = me.at(dx, dz)
        slot = w_ref.at[bx, bz, 2 * me.core + kind]
        if came is None:
            src = blocks_ref.at[2 * me.core + kind]
        else:
            coming.pop((kind, dx, dz, came)).wait_recv()
            src = slot
        for way in onward(kind, dx, dz):
            ddx, ddz = DIRS[way]
            coming[kind, dx - ddx, dz - ddz, way] = copies.start(src, slot, me.device(ddx, ddz))
        if came is not None:
            shared.append(copies.start(slot, slot, me.sibling))
    assert not coming
    for c in pats:
        c.wait_recv()
    pats = [copies.start(p_ref.at[x], p_ref.at[x], d) for d in line_x]
    for c in pats + shared:
        c.wait_recv()
    copies.finish()


def gather(blocks, pat):
    vmem = pl.BlockSpec(memory_space=pltpu.VMEM)
    return pl.pallas_call(
        gather_kernel,
        out_shape=(
            jax.ShapeDtypeStruct((X, Z, Q, BS, BS), BF16),
            jax.ShapeDtypeStruct((X, Z, 8, BS), I32),
        ),
        in_specs=[vmem, vmem],
        out_specs=(vmem, vmem),
        scratch_shapes=[pltpu.SemaphoreType.DMA((N_GATHER,))] * 2,
        compiler_params=pltpu.CompilerParams(
            collective_id=0, has_side_effects=True, vmem_limit_bytes=60 * 2**20),
        name="gather_blocks",
    )(blocks, pat)


GROUPS = (
    (0, 2, None), (1, None, 4), (1, None, 3), (1, None, -3), (0, 1, None), (0, -1, None),
    (1, None, 2), (1, None, -2), (1, None, 1), (1, None, -1), (0, 0, None), (1, None, 0),
)
SIZES = tuple(Z if g[2] is None else X for g in GROUPS)
STARTS = tuple(sum(SIZES[:i]) for i in range(len(SIZES)))
N_OWN = sum(SIZES)
ROWS_, COLS_, PREV_, LAST_, ROWEND_, SAME_ = range(6)
N_SUM = 12 + 2 * 5 + 7 + 3 + 4


def lanes(block):
    return pl.ds(pl.multiple_of(block * BS, BS), BS)


def main_kernel(meta, order, x_ref, og_ref, w_ref, rec_ref, wg_ref,
                xb, xt, ogb, pre, ag, ig_out, sib_out, sib_in, a_out, a_in1, a_in2, a_q, a_in3,
                b_out, b_in, b_q, b_in3, mine, theirs, send, recv, send_ig, recv_ig):
    me = Place()
    micro, tok = x_ref.shape[0], x_ref.shape[1]
    T = micro * tok
    n_rows = x_ref.shape[2] // BS
    line_z = [me.device(0, k) for k in range(1, Z)]
    line_x = [me.device(k, 0) for k in range(1, X)]
    meet(line_z + line_x + [me.sibling, me.twin, me.other_section])
    copies = Copies(send, recv)

    @pl.loop(0, n_rows)
    def _(r):
        block = x_ref[:, :, lanes(r)].reshape(T, BS)
        xb[r] = block
        xt[r] = block.T

    @pl.loop(0, og_ref.shape[2] // BS)
    def _(c):
        ogb[c] = og_ref[:, :, lanes(c)].reshape(T, BS)

    pre[NBLK] = jnp.zeros((micro, tok, BS), F32)

    U = 4

    @pl.loop(0, NBLK // U)
    def _(i):
        prods = []
        for u in range(U):
            b = i * U + u
            prods.append(jnp.dot(xb[meta[ROWS_, b]], w_ref[b], preferred_element_type=F32))
        for u in range(U):
            b = i * U + u
            pre[b] = prods[u].reshape(micro, tok, BS) + pre[meta[PREV_, b]]

    @pl.loop(0, NBLK)
    def _(b):
        v = pre[meta[LAST_, b]].reshape(T, BS)
        s = jax.nn.sigmoid(v)
        slope = s * (1.0 + v * (1.0 - s))
        og = ogb[meta[COLS_, b]].astype(F32)
        ag[b] = (og * slope).astype(BF16)

    to_other = pltpu.make_async_remote_copy(
        src_ref=ig_out, dst_ref=rec_ref, send_sem=send_ig, recv_sem=recv_ig,
        device_id=me.other_section, device_id_type=MESH)

    @pl.when(me.section == 1)
    def _():
        @pl.loop(0, NBLK // U)
        def _(i):
            prods = []
            for u in range(U):
                b = i * U + u
                prods.append(lax.dot_general(
                    ag[b], w_ref[b], (((1,), (1,)), ((), ())), preferred_element_type=F32))
            for u in range(U):
                b = i * U + u
                pre[b] = prods[u].reshape(micro, tok, BS) + pre[meta[SAME_, b]]

        @pl.loop(0, n_rows)
        def _(r):
            end = meta[ROWEND_, r]
            for i in range(micro):
                ig_out[i, :, lanes(r)] = pre[end, order[i]].astype(BF16)

        to_other.start()

        @pl.loop(0, micro)
        def _(i):
            rec_ref[i] = jnp.zeros(rec_ref.shape[1:], BF16)

    def block_of(group, k, core):
        kind, dx, dz = GROUPS[group]
        x, z = me.at(k if dx is None else dx, k - Z if dz is None else dz)
        return (x * Z + z) * Q + 2 * core + kind

    def product(b):
        return jnp.dot(xt[meta[ROWS_, b]], ag[b], preferred_element_type=F32)

    shared = []

    def share(g):
        @pl.loop(0, SIZES[g] // 4)
        def _(i):
            for u in range(4):
                k = i * 4 + u
                sib_out[STARTS[g] + k] = product(block_of(g, k, 1 - me.core)).astype(BF16)

        at = pl.ds(STARTS[g], SIZES[g])
        shared.append(copies.start(sib_out.at[at], sib_in.at[at], me.sibling))

    def summed(g, k):
        return product(block_of(g, k, me.core)) + sib_in[STARTS[g] + k].astype(F32)

    def a_slice(direction, n):
        return pl.ds(direction * Z, n)

    sent = {}

    def own(g):
        kind, dx, dz = GROUPS[g]
        shared[g].wait_recv()
        if kind == 0 and dx == 2:
            @pl.loop(0, Z // 4)
            def _(i):
                for u in range(4):
                    a_out[2 * Z + i * 4 + u] = summed(g, i * 4 + u).astype(BF16)
            sent["a2+"] = copies.start(a_out.at[pl.ds(2 * Z, 4)], a_in1.at[pl.ds(0, 4)], me.device(1, 0))
            sent["a2-"] = copies.start(a_out.at[pl.ds(2 * Z + 4, 4)], a_in1.at[pl.ds(4, 4)], me.device(-1, 0))
        elif kind == 0 and dx != 0:
            side = 0 if dx > 0 else 1
            sent["a2+" if dx > 0 else "a2-"].wait_recv()
            for half in range(2):
                for u in range(4):
                    k = half * 4 + u
                    v = summed(g, k)
                    if half == side:
                        v = v + a_in1[k].astype(F32)
                    a_out[side * Z + k] = v.astype(BF16)
            at = pl.ds(side * Z, Z)
            sent["a1", side] = copies.start(a_out.at[at], a_in2.at[at], me.device(dx, 0))
        elif kind == 0:
            sent["a1", 0].wait_recv()
            sent["a1", 1].wait_recv()

            @pl.loop(0, Z // 4)
            def _(i):
                for u in range(4):
                    k = i * 4 + u
                    v = summed(g, k) + (a_in2[k].astype(F32) + a_in2[Z + k].astype(F32))
                    a_q[k] = v.astype(BF16)
                    if u == 0:
                        @pl.when(i == 0)
                        def _():
                            mine[0] = v
            for k in range(1, Z):
                sent["a0", k] = copies.start(a_q.at[k], a_in3.at[k], me.device(0, k))
        elif dz == 4:
            for k in range(4):
                b_out[3 * 8 + k] = summed(g, k).astype(BF16)
            for side in range(2):
                at = pl.ds(3 * 8 + 2 * side, 2)
                sent["b", 4, side] = copies.start(b_out.at[at], b_in.at[at], me.device(0, 1 - 2 * side))
        elif dz != 0:
            side, far = (0 if dz > 0 else 1), abs(dz)
            sent["b", far + 1, side].wait_recv()
            for k in range(4):
                v = summed(g, k)
                if far < 3:
                    v = v + b_in[far * 8 + side * 4 + k].astype(F32)
                elif k // 2 == side:
                    v = v + b_in[3 * 8 + k].astype(F32)
                b_out[(far - 1) * 8 + side * 4 + k] = v.astype(BF16)
            at = pl.ds((far - 1) * 8 + side * 4, 4)
            sent["b", far, side] = copies.start(b_out.at[at], b_in.at[at], me.device(0, 1 - 2 * side))
        else:
            sent["b", 1, 0].wait_recv()
            sent["b", 1, 1].wait_recv()
            for k in range(4):
                v = summed(g, k) + (b_in[k].astype(F32) + b_in[4 + k].astype(F32))
                if k == 0:
                    mine[1] = v
                else:
                    b_q[k] = v.astype(BF16)
            for k in range(1, X):
                sent["b0", k] = copies.start(b_q.at[k], b_in3.at[k], me.device(k, 0))

    lead = 2
    for g in range(len(GROUPS) + lead):
        if g < len(GROUPS):
            share(g)
        if g >= lead:
            own(g - lead)

    total_a, total_b = mine[0], mine[1]
    for k in range(1, Z):
        sent["a0", k].wait_recv()
        total_a += a_in3[k].astype(F32)
    for k in range(1, X):
        sent["b0", k].wait_recv()
        total_b += b_in3[k].astype(F32)
    theirs[0] = total_a.astype(BF16)
    theirs[1] = total_b.astype(BF16)
    crossing = copies.start(theirs.at[pl.ds(0, 2)], theirs.at[pl.ds(2, 2)], me.twin)
    crossing.wait_recv()
    scale = 1.0 / 128.0
    own_pair = pl.ds(2 * me.core, 2)
    wg_ref[own_pair] = (theirs[0:2].astype(F32) + theirs[2:4].astype(F32)) * scale
    last = copies.start(wg_ref.at[own_pair], wg_ref.at[own_pair], me.sibling)
    last.wait_recv()
    copies.finish()

    @pl.when(me.section == 1)
    def _():
        to_other.wait_send()

    @pl.when(me.section == 0)
    def _():
        to_other.wait_recv()


def finish(meta, order, x, og, w):
    vmem = pl.BlockSpec(memory_space=pltpu.VMEM)
    smem = pl.BlockSpec(memory_space=pltpu.SMEM)
    micro, tok, d = x.shape
    T = micro * tok

    def blocks(n, kind=BF16):
        return pltpu.VMEM((n, BS, BS), kind)

    return pl.pallas_call(
        main_kernel,
        out_shape=(
            jax.ShapeDtypeStruct(x.shape, BF16),
            jax.ShapeDtypeStruct((Q, BS, BS), F32),
        ),
        in_specs=[smem, smem, vmem, vmem, vmem],
        out_specs=(vmem, vmem),
        scratch_shapes=[
            pltpu.VMEM((d // BS, T, BS), BF16),
            pltpu.VMEM((d // BS, BS, T), BF16),
            pltpu.VMEM((og.shape[2] // BS, T, BS), BF16),
            pltpu.VMEM((NBLK + 1, micro, tok, BS), F32),
            pltpu.VMEM((NBLK, T, BS), BF16),
            pltpu.VMEM(x.shape, BF16),
            blocks(N_OWN), blocks(N_OWN),
            blocks(3 * Z), blocks(Z), blocks(2 * Z), blocks(Z), blocks(Z),
            blocks(28), blocks(28), blocks(4), blocks(4),
            blocks(2, F32), blocks(4),
            pltpu.SemaphoreType.DMA((N_SUM,)), pltpu.SemaphoreType.DMA((N_SUM,)),
            pltpu.SemaphoreType.DMA, pltpu.SemaphoreType.DMA,
        ],
        compiler_params=pltpu.CompilerParams(
            collective_id=1, has_side_effects=True, vmem_limit_bytes=60 * 2**20),
        name="gradients",
    )(meta, order, x, og, w)


def tables(pats):
    pats = pats[:, :, :Q, :2].reshape(NBLK, 2)
    rows, cols = pats[:, 0], pats[:, 1]
    number = jnp.arange(NBLK, dtype=I32)
    alike = cols[:, None] == cols[None, :]
    earlier = number[:, None] < number[None, :]
    prev = jnp.max(jnp.where(alike & earlier, number[:, None], -1), axis=0)
    prev = jnp.where(prev < 0, NBLK, prev)
    last = jnp.max(jnp.where(alike, number[:, None], -1), axis=0)
    row_end = jnp.max(jnp.where(rows[:, None] == number[None, :], number[:, None], -1), axis=0)
    row_end = jnp.where(row_end < 0, NBLK, row_end)
    same = jnp.max(jnp.where((rows[:, None] == rows[None, :]) & earlier, number[:, None], -1), axis=0)
    same = jnp.where(same < 0, NBLK, same)
    return jnp.stack([rows, cols, prev, last, row_end, same])


def local(activations, out_grad, blocks, pattern, order):
    pat = jnp.pad(pattern[0], ((0, 8 - Q), (0, BS - 2)))
    w, pats = gather(blocks[0], pat)
    meta = tables(pats)
    received, weight_grad = finish(
        meta, order, activations[0], out_grad[0], w.reshape(NBLK, BS, BS))
    return received[None], weight_grad[None]


def solution(mesh):
    in_specs = (
        P("section", None, ("fsdp", "dp"), None),
        P("section", None, ("fsdp", "dp"), None),
        P("section", "fsdp", None, None),
        P("section", "fsdp", None),
        P(),
    )
    out_specs = (P("section", None, ("fsdp", "dp"), None), P("section", "fsdp", None, None))
    return jax.shard_map(local, mesh=mesh, in_specs=in_specs, out_specs=out_specs, check_vma=False)
```

time: 447 us -> 113 us (0.25)
  waiting for transfers between devices: 255 us -> 0 us
  Pallas kernels: 0 us -> 105 us
  other arithmetic: 63 us -> 0.24 us
  blocking collectives: 40.6 us -> 0 us
  local copies, waits for them, and re-layouts: 43.9 us -> 6.94 us
  matrix products: 25.1 us -> 0 us
  between operations: 13.8 us -> 0.67 us
    reduce_scatter x1 -> x0, waiting for transfers between devices: 172 us -> none  [local(): lax.psum_scatter(jnp.einsum('tbk,tbn->bkn', rows_in, cols_in, preferred_e...]
    pallas_call x0 -> x2, Pallas kernels: none -> 105 us  [the longest x1 65.7 us: finish(): pl.pallas_call(main_kernel, out_shape=(jax.ShapeDtypeStruct(x.shape, BF16...]
    scatter-add x8 -> x0, other arithmetic: 50.4 us -> none  [the longest x4 25.4 us: backward_step(): return running.at[:, indices[:, 0]].add(product)]
    psum x1 -> x0, waiting for transfers between devices: 50.4 us -> none  [local(): summed = lax.psum(owned_grads, 'dp')]
    all_gather x1 -> x0, blocking collectives: 40.6 us -> none  [local(): all_indices = lax.all_gather(pattern[0], 'fsdp', axis=0, tiled=True)]
    all_gather x1 -> x0, waiting for transfers between devices: 31.9 us -> none  [local(): lax.all_gather(own_blocks, 'fsdp', axis=0, tiled=True)]
    gather x11 -> x0, local copies, waits for them, and re-layouts: 26.8 us -> none  [the longest x4 11.2 us: backward_step(): cols_in = jnp.take(grad_cols, indices[:, 1], axis=1)]
    dot_general x9 -> x0, matrix products: 25.1 us -> none  [the longest x1 8.5 us: local(): jnp.einsum('tbk,tbn->bkn', rows_in, cols_in, preferred_element_type=jnp.f...]
  transfers between devices with their start and end apart: 4 -> 0, of which waited for: 3 -> 0; matrix products, arithmetic and copies ran while one was open for 14% -> 0% of each run, Pallas kernels for 0% -> 0%
where the time goes in v1:
time: 113 us
  Pallas kernels  105 us (93%)
  local copies, waits for them, and re-layouts  6.94 us (6%)
    pallas_call x1, Pallas kernels, finish(): pl.pallas_call(main_kernel, out_shape=(jax.ShapeDtypeStruct(x.shape, BF16...  65.7 us
    pallas_call x1, Pallas kernels, gather(): pl.pallas_call(gather_kernel, out_shape=(jax.ShapeDtypeStruct((X, Z, Q, B...  39.4 us
    unnamed x4, local copies, waits for them, and re-layouts  3.97 us

profile of v1, /device:TPU:9, one launch (start us, length us, event | category | flops | bytes accessed | tf_op | source)
XLA Modules:
  0.0 113.0 jit_solution(7406971988283698013)
XLA Ops:
  0.6 0.8 copy.10
  1.4 0.6 pad.4.pat_ref
  2.0 39.4 %gather_blocks.1 = (bf16[4,8,4,128,128]{4,3,2,1,0:T(8,128)(2,1)}, s32[4,8,8,128]{3,2,1,0:T(8,128)}) custom-call(bf16[4,128,128]{2,1,0:T(8,128)(2,1)} %bitcast.25, s32[8,128]{1,0:T(8,128)} %pad.4.pat_ref), custom_call_target="tpu_custom_call" | custom-call | tf_op jit(solution)/shard_map/gather_blocks/pallas_call | solution.py:151
  41.5 0.9 slice.9
  42.4 0.1 fusion.2
  42.4 0.1 copy.14
  42.5 0.1 copy.13
  42.6 0.1 select_reduce_fusion
  42.7 0.1 fusion
  42.8 0.6 stack.10.meta
  43.5 65.7 %gradients.1 = (bf16[4,32,3584]{2,1,0:T(8,128)(2,1)}, f32[4,128,128]{2,1,0:T(8,128)}) custom-call(s32[6,128]{1,0:T(8,128)} %stack.10.meta, s32[4]{0:T(128)} %order.1, bf16[4,32,3584]{2,1,0:T(8,128)(2,1)} %bitcast.22, bf16[4,32,14336]{2,1,0:T(8,128)(2,1)} %bitcast.20, bf16[128,128,128]{2,1,0:T(8,128)(2,1)} %bitcast.19), custom_call_target="tpu_custom_call" | custom-call | tf_op jit(solution)/shard_map/gradients/pallas_call | solution.py:393
  109.2 2.2 %copy.17 = bf16[1,4,32,3584]{3,2,1,0:T(8,128)(2,1)} copy(bf16[1,4,32,3584]{3,2,1,0:T(8,128)(2,1)} %bitcast.21) | data formatting | bytes 1835008
  111.3 1.7 %copy.18 = f32[1,4,128,128]{3,2,1,0:T(8,128)} copy(f32[1,4,128,128]{3,2,1,0:T(8,128)} %bitcast.24) | data formatting | bytes 524288
  (2 shorter events, 0.0 us)

commit v2 on v0

v2 whole, which is shorter than its diff:
```python
import jax
import jax.numpy as jnp
from jax import lax
from jax.experimental import pallas as pl
from jax.experimental.pallas import tpu as pltpu
from jax.sharding import PartitionSpec as P

MESH = pl.DeviceIdType.MESH
X, Z = 4, 8
Q = 4
BS = 128
NBLK = X * Z * Q
PAIR = 2 * BS
A_ROWS = 208
B_ROWS = PAIR - A_ROWS
F32, BF16, I32 = jnp.float32, jnp.bfloat16, jnp.int32
NEAR_X = (1, -1, 2)
NEAR_Z = (1, -1, 2, -2, 3, -3, 4)
IN_GROUPS = (0,) + NEAR_Z
OUT_GROUPS = (4, 3, -3, 2, -2, 1, -1, 0)
ROWS_, COLS_, PREV_, LAST_, ROW_PREV_, ROW_END_ = range(6)
N_COPIES = 7 + 3 + 62 + 8 + 8 + 24 + 7 + 7 + 3 + 2


class Place:
    def __init__(self):
        fsdp, dp = lax.axis_index("fsdp"), lax.axis_index("dp")
        self.x, self.z = fsdp // Z, lax.rem(fsdp, Z)
        self.core = lax.rem(dp, 2)
        self.section = lax.axis_index("section")
        self.sibling = {"dp": dp + 1 - 2 * self.core}
        self.twin = {"dp": lax.rem(dp + 2, 4)}
        self.other_section = {"section": 1 - self.section}

    def at(self, dx, dz):
        return lax.rem(self.x + dx + X, X), lax.rem(self.z + dz + Z, Z)

    def device(self, dx, dz):
        x, z = self.at(dx, dz)
        return {"fsdp": x * Z + z}


class Copies:
    def __init__(self, send, recv):
        self.send, self.recv, self.used, self.made = send, recv, 0, []

    def start(self, src, dst, device):
        n = self.used
        self.used += 1
        copy = pltpu.make_async_remote_copy(
            src_ref=src, dst_ref=dst, send_sem=self.send.at[n], recv_sem=self.recv.at[n],
            device_id=device, device_id_type=MESH)
        copy.start()
        self.made.append(copy)
        return copy

    def finish(self):
        for copy in self.made:
            copy.wait_send()


def meet(devices):
    barrier = pltpu.get_barrier_semaphore()
    for device in devices:
        pl.semaphore_signal(barrier, inc=1, device_id=device, device_id_type=MESH)
    pl.semaphore_wait(barrier, len(devices))


def lanes(block):
    return pl.ds(pl.multiple_of(block * BS, BS), BS)


def make_tables(me, p_all, m_rows, m_cols, table):
    for x in range(X):
        for z in range(Z):
            at = pl.ds((x * Z + z) * Q, Q)
            m_rows[at, :] = p_all[x, z, 0:Q, :]
            m_cols[at, :] = p_all[x, z, Q:2 * Q, :]
    rows, cols = m_rows[...], m_cols[...]
    rows_t, cols_t = rows.T, cols.T
    number = lax.broadcasted_iota(I32, (NBLK, BS), 0)
    number_t = lax.broadcasted_iota(I32, (NBLK, BS), 1)

    def place(n):
        chip = n // Q
        d = (chip % Z - me.z + Z) % Z
        group = jnp.where(d == 0, 0, jnp.where(d <= Z // 2, 2 * d - 1, 2 * (Z - d)))
        return group * (X * Q) + (chip // Z) * Q + n % Q

    slot, slot_t = place(number), place(number_t)

    def latest(mask, value):
        return jnp.max(jnp.where(mask, value, -1), axis=0, keepdims=True)

    def or_none(best):
        return jnp.where(best < 0, NBLK, best)

    same_col, same_row = cols == cols_t, rows == rows_t
    table[...] = jnp.zeros(table.shape, I32)
    table[ROWS_:ROWS_ + 1, :] = rows_t[0:1, :]
    table[COLS_:COLS_ + 1, :] = cols_t[0:1, :]
    table[PREV_:PREV_ + 1, :] = or_none(latest(same_col & (slot < slot_t), slot))
    table[LAST_:LAST_ + 1, :] = latest(same_col, slot)
    table[ROW_PREV_:ROW_PREV_ + 1, :] = or_none(latest(same_row & (number < number_t), number))
    table[ROW_END_:ROW_END_ + 1, :] = or_none(latest(rows == number_t, number))


def kernel(pat_ref, order, blocks_ref, x_hbm, og_hbm, rec_ref, wg_ref,
           w, p_all, m_rows, m_cols, table, meta, x_v, og_v, xb, xt, ogb, pre, ag, ig_out,
           sib_out, sib_in, sa, ra, va, qa, ra2, sb, rb, vb, qb, rb2, mine, halves,
           send, recv, send_ig, recv_ig, load):
    me = Place()
    micro, tok = x_v.shape[0], x_v.shape[1]
    T = micro * tok
    n_rows, n_cols = x_v.shape[2] // BS, og_v.shape[2] // BS
    load_x = pltpu.make_async_copy(x_hbm, x_v, load.at[0])
    load_og = pltpu.make_async_copy(og_hbm, og_v, load.at[1])
    load_x.start()
    load_og.start()

    x, z = me.at(0, 0)
    w[x, z] = blocks_ref[...]
    p_all[x, z] = pat_ref[...]
    meet([me.device(0, k) for k in range(1, Z)] + [me.device(k, 0) for k in range(1, X)]
         + [me.sibling, me.twin, me.other_section])
    copies = Copies(send, recv)

    first_row = pl.multiple_of(me.core * PAIR, PAIR)
    part = {"a": pl.ds(first_row, A_ROWS), "b": pl.ds(first_row + A_ROWS, B_ROWS)}
    coming = {}

    def pass_on(kind, dx, dz, ex, ez):
        bx, bz = me.at(dx, dz)
        dst = w.at[bx, bz, part[kind]]
        src = blocks_ref.at[part[kind]] if dx == dz == 0 else dst
        there = (dx - ex + 1) % X - 1, (dz - ez + 3) % Z - 3
        coming[(kind, *there)] = copies.start(src, dst, me.device(ex, ez))

    def arrive(kind, dx, dz):
        coming.pop((kind, dx, dz)).wait_recv()

    pats = [copies.start(pat_ref, p_all.at[x, z], me.device(0, k)) for k in NEAR_Z]
    for j in NEAR_X:
        pass_on("b", 0, 0, j, 0)
    for k in NEAR_Z:
        pass_on("a", 0, 0, 0, k)
    for j in NEAR_X:
        pass_on("a", 0, 0, j, 0)
    for k in NEAR_Z:
        pass_on("b", 0, 0, 0, k)

    load_x.wait()

    @pl.loop(0, n_rows)
    def _(r):
        block = x_v[:, :, lanes(r)].reshape(T, BS)
        xb[r] = block
        xt[r] = block.T

    for c in pats:
        c.wait_recv()
    pats = [copies.start(p_all.at[x], p_all.at[x], me.device(j, 0)) for j in NEAR_X]

    for kind, d in (("b", 1), ("b", -1), ("a", 1), ("a", -1), ("b", 2), ("a", 2), ("a", -2)):
        if kind == "b":
            arrive("b", d, 0)
            for k in NEAR_Z:
                pass_on("b", d, 0, 0, k)
        else:
            arrive("a", 0, d)
            for j in NEAR_X:
                pass_on("a", 0, d, j, 0)

    for c in pats:
        c.wait_recv()
    make_tables(me, p_all, m_rows, m_cols, table)
    to_scalars = pltpu.make_async_copy(table, meta, load.at[2])
    to_scalars.start()

    for d in (3, -3, 4):
        arrive("a", 0, d)
        for j in NEAR_X:
            pass_on("a", 0, d, j, 0)

    load_og.wait()

    @pl.loop(0, n_cols)
    def _(c):
        ogb[c] = og_v[:, :, lanes(c)].reshape(T, BS)

    pre[NBLK] = jnp.zeros((micro, tok, BS), F32)
    to_scalars.wait()

    U = 8
    pair_rows = pl.ds(first_row, PAIR)
    shared = []

    def share_line(g):
        dz = IN_GROUPS[g]
        for dx in (0,) + NEAR_X:
            if dx != 0:
                arrive("a", dx, dz)
            if dz != 0:
                arrive("b", dx, dz)
        at = w.at[:, me.at(0, dz)[1], pair_rows]
        shared.append(copies.start(at, at, me.sibling))

    def forward_line(g):
        shared[g].wait_recv()
        bz = me.at(0, IN_GROUPS[g])[1]

        @pl.loop(0, X * Q // U)
        def _(i):
            prods = []
            for u in range(U):
                bx, q = i * (U // Q) + u // Q, u % Q
                b = (bx * Z + bz) * Q + q
                prods.append((b, jnp.dot(
                    xb[meta[ROWS_, b]], w[bx, bz, q * BS:(q + 1) * BS, :], preferred_element_type=F32)))
            for u, (b, prod) in enumerate(prods):
                pre[g * X * Q + i * U + u] = prod.reshape(micro, tok, BS) + pre[meta[PREV_, b]]

    for g in range(len(IN_GROUPS) + 1):
        if g < len(IN_GROUPS):
            share_line(g)
        if g > 0:
            forward_line(g - 1)
    assert not coming

    @pl.loop(0, NBLK // 2)
    def _(i):
        for u in range(2):
            b = i * 2 + u
            v = pre[meta[LAST_, b]].reshape(T, BS)
            s = jax.nn.sigmoid(v)
            slope = s * (1.0 + v * (1.0 - s))
            ag[b] = (ogb[meta[COLS_, b]].astype(F32) * slope).astype(BF16)

    to_other = pltpu.make_async_remote_copy(
        src_ref=ig_out, dst_ref=rec_ref, send_sem=send_ig, recv_sem=recv_ig,
        device_id=me.other_section, device_id_type=MESH)

    @pl.when(me.section == 1)
    def _():
        @pl.loop(0, NBLK // U)
        def _(i):
            prods = []
            for u in range(U):
                b = i * U + u
                weight = w[b // (Z * Q), (b // Q) % Z, pl.ds(pl.multiple_of((b % Q) * BS, BS), BS), :]
                prods.append(lax.dot_general(
                    ag[b], weight, (((1,), (1,)), ((), ())), preferred_element_type=F32))
            for u in range(U):
                b = i * U + u
                pre[b] = prods[u].reshape(micro, tok, BS) + pre[meta[ROW_PREV_, b]]

        @pl.loop(0, n_rows)
        def _(r):
            end = meta[ROW_END_, r]
            for i in range(micro):
                ig_out[i, :, lanes(r)] = pre[end, order[i]].astype(BF16)

        to_other.start()

        @pl.loop(0, micro)
        def _(i):
            rec_ref[i] = jnp.zeros(rec_ref.shape[1:], BF16)

    def product(dx, dz, q):
        bx, bz = me.at(dx, dz)
        b = (bx * Z + bz) * Q + q
        return jnp.dot(xt[meta[ROWS_, b]], ag[b], preferred_element_type=F32)

    halved = []

    def share(g):
        for dx in range(X):
            for q in range(2):
                p = product(dx, OUT_GROUPS[g], 2 * (1 - me.core) + q)
                sib_out[g, dx, q * BS:(q + 1) * BS, :] = p.astype(BF16)
        halved.append(copies.start(sib_out.at[g], sib_in.at[g], me.sibling))

    sent = {}

    def own(g):
        dz = OUT_GROUPS[g]
        halved[g].wait_recv()
        cut = A_ROWS - BS
        for dx in (2, 1, 3, 0):
            first = product(dx, dz, 2 * me.core) + sib_in[g, dx, 0:BS, :].astype(F32)
            second = product(dx, dz, 2 * me.core + 1) + sib_in[g, dx, BS:PAIR, :].astype(F32)
            if dx != 0:
                sa[dx - 1, g, 0:BS, :] = first.astype(BF16)
                sa[dx - 1, g, BS:A_ROWS, :] = second[:cut].astype(BF16)
                sent["a", dx, g] = copies.start(
                    sa.at[dx - 1, g], ra.at[dx - 1, g], me.device(dx, 0))
            else:
                va[g, 0:BS, :] = first
                va[g, BS:A_ROWS, :] = second[:cut]
            if dz != 0:
                sb[g, dx] = second[cut:].astype(BF16)
            else:
                vb[dx] = second[cut:]
        if dz != 0:
            sent["b", g] = copies.start(sb.at[g], rb.at[g], me.device(0, dz))

    def second_a(g):
        dz = OUT_GROUPS[g]
        for dx in range(1, X):
            sent["a", dx, g].wait_recv()
        total = va[g] + (ra[0, g].astype(F32) + ra[1, g].astype(F32) + ra[2, g].astype(F32))
        if dz != 0:
            qa[g] = total.astype(BF16)
            sent["a2", g] = copies.start(qa.at[g], ra2.at[g], me.device(0, dz))
        else:
            mine[0:A_ROWS, :] = total

    def second_b():
        for g, dz in enumerate(OUT_GROUPS):
            if dz != 0:
                sent["b", g].wait_recv()
        for dx in (2, 1, 3, 0):
            total = vb[dx]
            for g, dz in enumerate(OUT_GROUPS):
                if dz != 0:
                    total += rb[g, dx].astype(F32)
            if dx != 0:
                qb[dx] = total.astype(BF16)
                sent["b2", dx] = copies.start(qb.at[dx], rb2.at[dx], me.device(dx, 0))
            else:
                mine[A_ROWS:PAIR, :] = total

    n = len(OUT_GROUPS)
    for g in range(n + 5):
        if g < n:
            share(g)
        if 2 <= g < n + 2:
            own(g - 2)
        if g == n + 4:
            second_b()
        if g >= 5:
            second_a(g - 5)

    total_a, total_b = mine[0:A_ROWS, :], mine[A_ROWS:PAIR, :]
    for g, dz in enumerate(OUT_GROUPS):
        if dz != 0:
            sent["a2", g].wait_recv()
            total_a += ra2[g].astype(F32)
    for dx in range(1, X):
        sent["b2", dx].wait_recv()
        total_b += rb2[dx].astype(F32)
    halves[0, 0:A_ROWS, :] = total_a.astype(BF16)
    halves[0, A_ROWS:PAIR, :] = total_b.astype(BF16)
    copies.start(halves.at[0], halves.at[1], me.twin).wait_recv()
    scale = 1.0 / 128.0
    wg_ref[pair_rows, :] = (halves[0].astype(F32) + halves[1].astype(F32)) * scale
    copies.start(wg_ref.at[pair_rows], wg_ref.at[pair_rows], me.sibling).wait_recv()
    copies.finish()

    @pl.when(me.section == 1)
    def _():
        to_other.wait_send()

    @pl.when(me.section == 0)
    def _():
        to_other.wait_recv()


def gradients(pat, order, blocks, x, og):
    vmem = pl.BlockSpec(memory_space=pltpu.VMEM)
    smem = pl.BlockSpec(memory_space=pltpu.SMEM)
    hbm = pl.BlockSpec(memory_space=pl.ANY)
    micro, tok, d = x.shape
    T = micro * tok
    n_rows, n_cols = d // BS, og.shape[2] // BS
    n = len(OUT_GROUPS)
    V = pltpu.VMEM
    return pl.pallas_call(
        kernel,
        out_shape=(
            jax.ShapeDtypeStruct(x.shape, BF16),
            jax.ShapeDtypeStruct((Q * BS, BS), F32),
        ),
        in_specs=[vmem, smem, vmem, hbm, hbm],
        out_specs=(vmem, vmem),
        scratch_shapes=[
            V((X, Z, Q * BS, BS), BF16),
            V((X, Z, 2 * Q, BS), I32),
            V((NBLK, BS), I32), V((NBLK, BS), I32), V((8, BS), I32),
            pltpu.SMEM((8, BS), I32),
            V(x.shape, BF16), V(og.shape, BF16),
            V((n_rows, T, BS), BF16), V((n_rows, BS, T), BF16), V((n_cols, T, BS), BF16),
            V((NBLK + 1, micro, tok, BS), F32),
            V((NBLK, T, BS), BF16),
            V(x.shape, BF16),
            V((n, X, PAIR, BS), BF16), V((n, X, PAIR, BS), BF16),
            V((X - 1, n, A_ROWS, BS), BF16), V((X - 1, n, A_ROWS, BS), BF16),
            V((n, A_ROWS, BS), F32), V((n, A_ROWS, BS), BF16), V((n, A_ROWS, BS), BF16),
            V((n, X, B_ROWS, BS), BF16), V((n, X, B_ROWS, BS), BF16),
            V((X, B_ROWS, BS), F32), V((X, B_ROWS, BS), BF16), V((X, B_ROWS, BS), BF16),
            V((PAIR, BS), F32), V((2, PAIR, BS), BF16),
            pltpu.SemaphoreType.DMA((N_COPIES,)), pltpu.SemaphoreType.DMA((N_COPIES,)),
            pltpu.SemaphoreType.DMA, pltpu.SemaphoreType.DMA, pltpu.SemaphoreType.DMA((3,)),
        ],
        compiler_params=pltpu.CompilerParams(
            collective_id=0, has_side_effects=True, vmem_limit_bytes=60 * 2**20),
        name="gradients",
    )(pat, order, blocks, x, og)


def local(activations, out_grad, blocks, pattern, order):
    pat = jnp.broadcast_to(pattern[0].T.reshape(2 * Q, 1), (2 * Q, BS))
    received, weight_grad = gradients(
        pat, order, blocks[0].reshape(Q * BS, BS), activations[0], out_grad[0])
    return received[None], weight_grad.reshape(1, Q, BS, BS)


def solution(mesh):
    in_specs = (
        P("section", None, ("fsdp", "dp"), None),
        P("section", None, ("fsdp", "dp"), None),
        P("section", "fsdp", None, None),
        P("section", "fsdp", None),
        P(),
    )
    out_specs = (P("section", None, ("fsdp", "dp"), None), P("section", "fsdp", None, None))
    return jax.shard_map(local, mesh=mesh, in_specs=in_specs, out_specs=out_specs, check_vma=False)
```

time: 447 us -> 83.4 us (0.19)
  waiting for transfers between devices: 255 us -> 0 us
  Pallas kernels: 0 us -> 77.3 us
  other arithmetic: 63 us -> 0 us
  blocking collectives: 40.6 us -> 0 us
  local copies, waits for them, and re-layouts: 43.9 us -> 5.25 us
  matrix products: 25.1 us -> 0 us
  between operations: 13.8 us -> 0.64 us
    reduce_scatter x1 -> x0, waiting for transfers between devices: 172 us -> none  [local(): lax.psum_scatter(jnp.einsum('tbk,tbn->bkn', rows_in, cols_in, preferred_e...]
    pallas_call x0 -> x1, Pallas kernels: none -> 77.3 us  [gradients(): pl.pallas_call(kernel, out_shape=(jax.ShapeDtypeStruct(x.shape, BF16), ja...]
    scatter-add x8 -> x0, other arithmetic: 50.4 us -> none  [the longest x4 25.4 us: backward_step(): return running.at[:, indices[:, 0]].add(product)]
    psum x1 -> x0, waiting for transfers between devices: 50.4 us -> none  [local(): summed = lax.psum(owned_grads, 'dp')]
    all_gather x1 -> x0, blocking collectives: 40.6 us -> none  [local(): all_indices = lax.all_gather(pattern[0], 'fsdp', axis=0, tiled=True)]
    all_gather x1 -> x0, waiting for transfers between devices: 31.9 us -> none  [local(): lax.all_gather(own_blocks, 'fsdp', axis=0, tiled=True)]
    gather x11 -> x0, local copies, waits for them, and re-layouts: 26.8 us -> none  [the longest x4 11.2 us: backward_step(): cols_in = jnp.take(grad_cols, indices[:, 1], axis=1)]
    dot_general x9 -> x0, matrix products: 25.1 us -> none  [the longest x1 8.5 us: local(): jnp.einsum('tbk,tbn->bkn', rows_in, cols_in, preferred_element_type=jnp.f...]
  transfers between devices with their start and end apart: 4 -> 0, of which waited for: 3 -> 0; matrix products, arithmetic and copies ran while one was open for 14% -> 0% of each run, Pallas kernels for 0% -> 0%
where the time goes in v2:
time: 83.4 us; the launch traced here: 83.2 us
  Pallas kernels  77.3 us (93%)
  local copies, waits for them, and re-layouts  5.25 us (6%)
    pallas_call x1, Pallas kernels, gradients(): pl.pallas_call(kernel, out_shape=(jax.ShapeDtypeStruct(x.shape, BF16), ja...  77.3 us
    unnamed x2, local copies, waits for them, and re-layouts  3.83 us

profile of v2, /device:TPU:9, one launch (start us, length us, event | category | flops | bytes accessed | tf_op | source)
XLA Modules:
  0.0 83.2 jit_solution(1260923205866758276)
XLA Ops:
  0.6 0.8 broadcast_in_dim.10
  1.4 0.7 broadcast_in_dim.11.pat_ref
  2.1 77.3 %gradients.1 = (bf16[4,32,3584]{2,1,0:T(8,128)(2,1)}, f32[512,128]{1,0:T(8,128)}) custom-call(s32[8,128]{1,0:T(8,128)} %broadcast_in_dim.11.pat_ref, s32[4]{0:T(128)} %order.1, bf16[512,128]{1,0:T(8,128)(2,1)} %bitcast.12, bf16[4,32,3584]{2,1,0:T(8,128)(2,1)} %bitcast.10, bf16[4,32,14336]{2,1,0:T(8,128)(2,1)} %bitcast.8), custom_call_target="tpu_custom_call" | custom-call | tf_op jit(solution)/shard_map/gradients/pallas_call | solution.py:378
  79.4 2.2 %copy.9 = bf16[1,4,32,3584]{3,2,1,0:T(8,128)(2,1)} copy(bf16[1,4,32,3584]{3,2,1,0:T(8,128)(2,1)} %bitcast.9) | data formatting | bytes 1835008
  81.6 1.7 %copy.10 = f32[1,4,128,128]{3,2,1,0:T(8,128)} copy(f32[1,4,128,128]{3,2,1,0:T(8,128)} %bitcast.11) | data formatting | bytes 524288

commit v3 on v2

--- a/solution.py
+++ b/solution.py
@@ -11,7 +11,8 @@
 BS = 128
 NBLK = X * Z * Q
 PAIR = 2 * BS
-A_ROWS = 208
+A_IN = 208
+A_ROWS = 192
 B_ROWS = PAIR - A_ROWS
 F32, BF16, I32 = jnp.float32, jnp.bfloat16, jnp.int32
 NEAR_X = (1, -1, 2)
@@ -105,8 +106,8 @@
     table[ROW_END_:ROW_END_ + 1, :] = or_none(latest(rows == number_t, number))
 
 
-def kernel(pat_ref, order, blocks_ref, x_hbm, og_hbm, rec_ref, wg_ref,
-           w, p_all, m_rows, m_cols, table, meta, x_v, og_v, xb, xt, ogb, pre, ag, ig_out,
+def kernel(pat_hbm, order_hbm, blocks_hbm, x_hbm, og_hbm, rec_ref, wg_ref,
+           pat_ref, order, blocks_ref, w, p_all, m_rows, m_cols, table, meta, x_v, og_v, xb, xt, ogb, pre, ag, ig_out,
            sib_out, sib_in, sa, ra, va, qa, ra2, sb, rb, vb, qb, rb2, mine, halves,
            send, recv, send_ig, recv_ig, load):
     me = Place()
@@ -115,18 +116,23 @@
     n_rows, n_cols = x_v.shape[2] // BS, og_v.shape[2] // BS
     load_x = pltpu.make_async_copy(x_hbm, x_v, load.at[0])
     load_og = pltpu.make_async_copy(og_hbm, og_v, load.at[1])
-    load_x.start()
-    load_og.start()
+    loads = [pltpu.make_async_copy(src, dst, load.at[3 + i]) for i, (src, dst) in enumerate(
+        ((pat_hbm, pat_ref), (blocks_hbm, blocks_ref), (order_hbm, order)))]
+    for c in loads + [load_x, load_og]:
+        c.start()
+    for c in loads:
+        c.wait()
 
     x, z = me.at(0, 0)
     w[x, z] = blocks_ref[...]
-    p_all[x, z] = pat_ref[...]
+    for i in range(2 * Q):
+        p_all[x, z, i:i + 1, :] = jnp.full((1, BS), pat_ref[i // Q, i % Q], I32)
     meet([me.device(0, k) for k in range(1, Z)] + [me.device(k, 0) for k in range(1, X)]
          + [me.sibling, me.twin, me.other_section])
     copies = Copies(send, recv)
 
     first_row = pl.multiple_of(me.core * PAIR, PAIR)
-    part = {"a": pl.ds(first_row, A_ROWS), "b": pl.ds(first_row + A_ROWS, B_ROWS)}
+    part = {"a": pl.ds(first_row, A_IN), "b": pl.ds(first_row + A_IN, PAIR - A_IN)}
     coming = {}
 
     def pass_on(kind, dx, dz, ex, ez):
@@ -139,7 +145,7 @@
     def arrive(kind, dx, dz):
         coming.pop((kind, dx, dz)).wait_recv()
 
-    pats = [copies.start(pat_ref, p_all.at[x, z], me.device(0, k)) for k in NEAR_Z]
+    pats = [copies.start(p_all.at[x, z], p_all.at[x, z], me.device(0, k)) for k in NEAR_Z]
     for j in NEAR_X:
         pass_on("b", 0, 0, j, 0)
     for k in NEAR_Z:
@@ -161,7 +167,7 @@
         c.wait_recv()
     pats = [copies.start(p_all.at[x], p_all.at[x], me.device(j, 0)) for j in NEAR_X]
 
-    for kind, d in (("b", 1), ("b", -1), ("a", 1), ("a", -1), ("b", 2), ("a", 2), ("a", -2)):
+    for kind, d in (("b", 1), ("b", -1), ("a", 1), ("a", -1), ("b", 2), ("a", 2), ("a", -2), ("a", 3), ("a", -3), ("a", 4)):
         if kind == "b":
             arrive("b", d, 0)
             for k in NEAR_Z:
@@ -176,11 +182,6 @@
     make_tables(me, p_all, m_rows, m_cols, table)
     to_scalars = pltpu.make_async_copy(table, meta, load.at[2])
     to_scalars.start()
-
-    for d in (3, -3, 4):
-        arrive("a", 0, d)
-        for j in NEAR_X:
-            pass_on("a", 0, d, j, 0)
 
     load_og.wait()
 
@@ -240,31 +241,35 @@
         src_ref=ig_out, dst_ref=rec_ref, send_sem=send_ig, recv_sem=recv_ig,
         device_id=me.other_section, device_id_type=MESH)
 
-    @pl.when(me.section == 1)
-    def _():
-        @pl.loop(0, NBLK // U)
-        def _(i):
-            prods = []
-            for u in range(U):
-                b = i * U + u
-                weight = w[b // (Z * Q), (b // Q) % Z, pl.ds(pl.multiple_of((b % Q) * BS, BS), BS), :]
-                prods.append(lax.dot_general(
-                    ag[b], weight, (((1,), (1,)), ((), ())), preferred_element_type=F32))
-            for u in range(U):
-                b = i * U + u
-                pre[b] = prods[u].reshape(micro, tok, BS) + pre[meta[ROW_PREV_, b]]
-
-        @pl.loop(0, n_rows)
-        def _(r):
-            end = meta[ROW_END_, r]
-            for i in range(micro):
-                ig_out[i, :, lanes(r)] = pre[end, order[i]].astype(BF16)
-
-        to_other.start()
-
-        @pl.loop(0, micro)
-        def _(i):
-            rec_ref[i] = jnp.zeros(rec_ref.shape[1:], BF16)
+    def input_grad(first, n):
+        @pl.when(me.section == 1)
+        def _():
+            @pl.loop(first // U, (first + n) // U)
+            def _(i):
+                prods = []
+                for u in range(U):
+                    b = i * U + u
+                    weight = w[b // (Z * Q), (b // Q) % Z, pl.ds(pl.multiple_of((b % Q) * BS, BS), BS), :]
+                    prods.append(lax.dot_general(
+                        ag[b], weight, (((1,), (1,)), ((), ())), preferred_element_type=F32))
+                for u in range(U):
+                    b = i * U + u
+                    pre[b] = prods[u].reshape(micro, tok, BS) + pre[meta[ROW_PREV_, b]]
+
+    def send_input_grad():
+        @pl.when(me.section == 1)
+        def _():
+            @pl.loop(0, n_rows)
+            def _(r):
+                end = meta[ROW_END_, r]
+                for i in range(micro):
+                    ig_out[i, :, lanes(r)] = pre[end, order[i]].astype(BF16)
+
+            to_other.start()
+
+            @pl.loop(0, micro)
+            def _(i):
+                rec_ref[i] = jnp.zeros(rec_ref.shape[1:], BF16)
 
     def product(dx, dz, q):
         bx, bz = me.at(dx, dz)
@@ -336,6 +341,10 @@
             share(g)
         if 2 <= g < n + 2:
             own(g - 2)
+        if g < 4:
+            input_grad(g * (NBLK // 4), NBLK // 4)
+        if g == 4:
+            send_input_grad()
         if g == n + 4:
             second_b()
         if g >= 5:
@@ -368,8 +377,7 @@
 
 def gradients(pat, order, blocks, x, og):
     vmem = pl.BlockSpec(memory_space=pltpu.VMEM)
-    smem = pl.BlockSpec(memory_space=pltpu.SMEM)
-    hbm = pl.BlockSpec(memory_space=pl.ANY)
+    hbm = pl.BlockSpec(memory_space=pltpu.HBM)
     micro, tok, d = x.shape
     T = micro * tok
     n_rows, n_cols = d // BS, og.shape[2] // BS
@@ -381,9 +389,10 @@
             jax.ShapeDtypeStruct(x.shape, BF16),
             jax.ShapeDtypeStruct((Q * BS, BS), F32),
         ),
-        in_specs=[vmem, smem, vmem, hbm, hbm],
+        in_specs=[hbm] * 5,
         out_specs=(vmem, vmem),
         scratch_shapes=[
+            pltpu.SMEM(pat.shape, I32), pltpu.SMEM(order.shape, I32), V(blocks.shape, BF16),
             V((X, Z, Q * BS, BS), BF16),
             V((X, Z, 2 * Q, BS), I32),
             V((NBLK, BS), I32), V((NBLK, BS), I32), V((8, BS), I32),
@@ -400,18 +409,38 @@
             V((X, B_ROWS, BS), F32), V((X, B_ROWS, BS), BF16), V((X, B_ROWS, BS), BF16),
             V((PAIR, BS), F32), V((2, PAIR, BS), BF16),
             pltpu.SemaphoreType.DMA((N_COPIES,)), pltpu.SemaphoreType.DMA((N_COPIES,)),
-            pltpu.SemaphoreType.DMA, pltpu.SemaphoreType.DMA, pltpu.SemaphoreType.DMA((3,)),
+            pltpu.SemaphoreType.DMA, pltpu.SemaphoreType.DMA, pltpu.SemaphoreType.DMA((6,)),
         ],
         compiler_params=pltpu.CompilerParams(
-            collective_id=0, has_side_effects=True, vmem_limit_bytes=60 * 2**20),
+            collective_id=0, has_side_effects=True, vmem_limit_bytes=52 * 2**20),
         name="gradients",
     )(pat, order, blocks, x, og)
 
 
+def deliver_kernel(a_in, b_in, a_out, b_out, sem):
+    copies = [pltpu.make_async_copy(a_in, a_out, sem.at[0]), pltpu.make_async_copy(b_in, b_out, sem.at[1])]
+    for c in copies:
+        c.start()
+    for c in copies:
+        c.wait()
+
+
+def deliver(a, b):
+    hbm = pl.BlockSpec(memory_space=pl.ANY)
+    return pl.pallas_call(
+        deliver_kernel,
+        out_shape=(jax.ShapeDtypeStruct(a.shape, a.dtype), jax.ShapeDtypeStruct(b.shape, b.dtype)),
+        in_specs=[hbm, hbm],
+        out_specs=(hbm, hbm),
+        scratch_shapes=[pltpu.SemaphoreType.DMA((2,))],
+        compiler_params=pltpu.CompilerParams(vmem_limit_bytes=2**20),
+        name="deliver",
+    )(a, b)
+
+
 def local(activations, out_grad, blocks, pattern, order):
-    pat = jnp.broadcast_to(pattern[0].T.reshape(2 * Q, 1), (2 * Q, BS))
-    received, weight_grad = gradients(
-        pat, order, blocks[0].reshape(Q * BS, BS), activations[0], out_grad[0])
+    received, weight_grad = deliver(*gradients(
+        pattern[0].T, order, blocks[0].reshape(Q * BS, BS), activations[0], out_grad[0]))
     return received[None], weight_grad.reshape(1, Q, BS, BS)
 
 

time: 83.4 us -> 77.8 us (0.933)
  local copies, waits for them, and re-layouts: 5.25 us -> 2.23 us
  Pallas kernels: 77.3 us -> 74.7 us
    pallas_call x1, Pallas kernels: 77.3 us -> 73.7 us  [gradients(): pl.pallas_call(kernel, out_shape=(jax.ShapeDtypeStruct(x.shape, BF16), ja...]
    unnamed x2 -> x6, local copies, waits for them, and re-layouts: 3.83 us -> 2.23 us
    broadcast_in_dim x2 -> x0, local copies, waits for them, and re-layouts: 1.42 us -> none  [local(): pat = jnp.broadcast_to(pattern[0].T.reshape(2 * Q, 1), (2 * Q, BS))]
    pallas_call x0 -> x1, Pallas kernels: none -> 1.02 us  [deliver(): pl.pallas_call(deliver_kernel, out_shape=(jax.ShapeDtypeStruct(a.shape, a...]
where the time goes in v3:
time: 77.8 us; the launch traced here: 77.6 us
  Pallas kernels  74.7 us (96%)
  local copies, waits for them, and re-layouts  2.23 us (3%)
    pallas_call x1, Pallas kernels, gradients(): pl.pallas_call(kernel, out_shape=(jax.ShapeDtypeStruct(x.shape, BF16), ja...  73.7 us
    unnamed x6, local copies, waits for them, and re-layouts  2.23 us

profile of v3, /device:TPU:9, one launch (start us, length us, event | category | flops | bytes accessed | tf_op | source)
XLA Modules:
  0.0 77.6 jit_solution(5397883810985645254)
XLA Ops:
  0.6 0.0 copy-start
  0.6 0.9 %copy-done = bf16[1,4,128,128]{3,2,1,0:T(8,128)(2,1)S(1)} copy-done((bf16[1,4,128,128]{3,2,1,0:T(8,128)(2,1)S(1)}, bf16[1,4,128,128]{3,2,1,0:T(8,128)(2,1)}, u32[]{:S(2)}) %copy-start) | copy-done | bytes 131096
  1.5 0.0 copy-start.1
  1.5 0.7 copy-done.1
  2.2 0.0 copy-start.2
  2.2 0.7 copy-done.2
  2.9 73.7 %gradients.1 = (bf16[4,32,3584]{2,1,0:T(8,128)(2,1)S(1)}, f32[512,128]{1,0:T(8,128)S(1)}) custom-call(s32[2,4]{1,0:T(2,128)S(1)} %bitcast.9, s32[4]{0:T(128)S(1)} %copy-done.2, bf16[512,128]{1,0:T(8,128)(2,1)S(1)} %bitcast.8, bf16[4,32,3584]{2,1,0:T(8,128)(2,1)} %bitcast.11, bf16[4,32,14336]{2,1,0:T(8,128)(2,1)} %bitcast.10), custom_call_target="tpu_custom_call" | custom-call | tf_op jit(solution)/shard_map/gradients/pallas_call | solution.py:386
  76.6 1.0 %deliver.1 = (bf16[4,32,3584]{2,1,0:T(8,128)(2,1)}, f32[512,128]{1,0:T(8,128)}) custom-call(bf16[4,32,3584]{2,1,0:T(8,128)(2,1)S(1)} %get-tuple-element.6.a_in, f32[512,128]{1,0:T(8,128)S(1)} %get-tuple-element.7.b_in), custom_call_target="tpu_custom_call" | custom-call | tf_op jit(solution)/shard_map/deliver/pallas_call | solution.py:430
Async XLA Ops:
  0.6 0.9 %copy-start = (bf16[1,4,128,128]{3,2,1,0:T(8,128)(2,1)S(1)}, bf16[1,4,128,128]{3,2,1,0:T(8,128)(2,1)}, u32[]{:S(2)}) copy-start(bf16[1,4,128,128]{3,2,1,0:T(8,128)(2,1)} %param.7) | copy-start | bytes 393220
  1.5 0.7 copy-start.1
  2.2 0.7 copy-start.2

commit v4 on v3

--- a/solution.py
+++ b/solution.py
@@ -11,16 +11,18 @@
 BS = 128
 NBLK = X * Z * Q
 PAIR = 2 * BS
-A_IN = 208
+A_IN = 224
 A_ROWS = 192
 B_ROWS = PAIR - A_ROWS
 F32, BF16, I32 = jnp.float32, jnp.bfloat16, jnp.int32
 NEAR_X = (1, -1, 2)
 NEAR_Z = (1, -1, 2, -2, 3, -3, 4)
+TWIN = (1, 2)
 IN_GROUPS = (0,) + NEAR_Z
+LATE = 6
 OUT_GROUPS = (4, 3, -3, 2, -2, 1, -1, 0)
 ROWS_, COLS_, PREV_, LAST_, ROW_PREV_, ROW_END_ = range(6)
-N_COPIES = 7 + 3 + 62 + 8 + 8 + 24 + 7 + 7 + 3 + 2
+N_COPIES = 7 + 3 + 62 + 14 + 8 + 24 + 7 + 7 + 3 + 2
 
 
 class Place:
@@ -28,13 +30,14 @@
         fsdp, dp = lax.axis_index("fsdp"), lax.axis_index("dp")
         self.x, self.z = fsdp // Z, lax.rem(fsdp, Z)
         self.core = lax.rem(dp, 2)
+        self.flip = 1 - 2 * (dp // 2)
         self.section = lax.axis_index("section")
         self.sibling = {"dp": dp + 1 - 2 * self.core}
         self.twin = {"dp": lax.rem(dp + 2, 4)}
         self.other_section = {"section": 1 - self.section}
 
     def at(self, dx, dz):
-        return lax.rem(self.x + dx + X, X), lax.rem(self.z + dz + Z, Z)
+        return lax.rem(self.x + dx + X, X), lax.rem(self.z + self.flip * dz + Z, Z)
 
     def device(self, dx, dz):
         x, z = self.at(dx, dz)
@@ -60,11 +63,10 @@
             copy.wait_send()
 
 
-def meet(devices):
-    barrier = pltpu.get_barrier_semaphore()
+def announce(devices):
     for device in devices:
-        pl.semaphore_signal(barrier, inc=1, device_id=device, device_id_type=MESH)
-    pl.semaphore_wait(barrier, len(devices))
+        pl.semaphore_signal(
+            pltpu.get_barrier_semaphore(), inc=1, device_id=device, device_id_type=MESH)
 
 
 def lanes(block):
@@ -84,7 +86,7 @@
 
     def place(n):
         chip = n // Q
-        d = (chip % Z - me.z + Z) % Z
+        d = (me.flip * (chip % Z - me.z) + Z) % Z
         group = jnp.where(d == 0, 0, jnp.where(d <= Z // 2, 2 * d - 1, 2 * (Z - d)))
         return group * (X * Q) + (chip // Z) * Q + n % Q
 
@@ -111,6 +113,9 @@
            sib_out, sib_in, sa, ra, va, qa, ra2, sb, rb, vb, qb, rb2, mine, halves,
            send, recv, send_ig, recv_ig, load):
     me = Place()
+    others = ([me.device(0, k) for k in range(1, Z)] + [me.device(k, 0) for k in range(1, X)]
+              + [me.sibling, me.twin, me.other_section])
+    announce(others)
     micro, tok = x_v.shape[0], x_v.shape[1]
     T = micro * tok
     n_rows, n_cols = x_v.shape[2] // BS, og_v.shape[2] // BS
@@ -124,14 +129,14 @@
         c.wait()
 
     x, z = me.at(0, 0)
-    w[x, z] = blocks_ref[...]
+    first_row = pl.multiple_of(me.core * PAIR, PAIR)
+    pair_rows = pl.ds(first_row, PAIR)
+    w[x, z, pair_rows, :] = blocks_ref[pair_rows, :]
     for i in range(2 * Q):
         p_all[x, z, i:i + 1, :] = jnp.full((1, BS), pat_ref[i // Q, i % Q], I32)
-    meet([me.device(0, k) for k in range(1, Z)] + [me.device(k, 0) for k in range(1, X)]
-         + [me.sibling, me.twin, me.other_section])
+    pl.semaphore_wait(pltpu.get_barrier_semaphore(), len(others))
     copies = Copies(send, recv)
 
-    first_row = pl.multiple_of(me.core * PAIR, PAIR)
     part = {"a": pl.ds(first_row, A_IN), "b": pl.ds(first_row + A_IN, PAIR - A_IN)}
     coming = {}
 
@@ -167,15 +172,23 @@
         c.wait_recv()
     pats = [copies.start(p_all.at[x], p_all.at[x], me.device(j, 0)) for j in NEAR_X]
 
-    for kind, d in (("b", 1), ("b", -1), ("a", 1), ("a", -1), ("b", 2), ("a", 2), ("a", -2), ("a", 3), ("a", -3), ("a", 4)):
+    for kind, d in (("b", 1), ("b", -1), ("a", 1), ("a", -1), ("b", 2), ("a", 2), ("a", -2), ("twin", 1),
+                    ("a", 3), ("a", -3), ("a", 4), ("twin", 2)):
         if kind == "b":
             arrive("b", d, 0)
             for k in NEAR_Z:
                 pass_on("b", d, 0, 0, k)
+        elif kind == "a":
+            arrive("a", 0, d)
+            if -d not in TWIN:
+                for j in NEAR_X:
+                    pass_on("a", 0, d, j, 0)
         else:
-            arrive("a", 0, d)
             for j in NEAR_X:
-                pass_on("a", 0, d, j, 0)
+                arrive("a", j, d)
+                bx, bz = me.at(j, d)
+                at = w.at[bx, bz, part["a"]]
+                coming["a", j, -d] = copies.start(at, at, me.twin)
 
     for c in pats:
         c.wait_recv()
@@ -192,22 +205,27 @@
     pre[NBLK] = jnp.zeros((micro, tok, BS), F32)
     to_scalars.wait()
 
-    U = 8
-    pair_rows = pl.ds(first_row, PAIR)
-    shared = []
+    U = 16
+    shared = [[] for _ in IN_GROUPS]
 
     def share_line(g):
         dz = IN_GROUPS[g]
         for dx in (0,) + NEAR_X:
-            if dx != 0:
+            if dx != 0 and dz not in TWIN:
                 arrive("a", dx, dz)
             if dz != 0:
                 arrive("b", dx, dz)
-        at = w.at[:, me.at(0, dz)[1], pair_rows]
-        shared.append(copies.start(at, at, me.sibling))
+            if g >= LATE:
+                bx, bz = me.at(dx, dz)
+                at = w.at[bx, bz, pair_rows]
+                shared[g].append(copies.start(at, at, me.sibling))
+        if g < LATE:
+            at = w.at[:, me.at(0, dz)[1], pair_rows]
+            shared[g].append(copies.start(at, at, me.sibling))
 
     def forward_line(g):
-        shared[g].wait_recv()
+        for c in shared[g]:
+            c.wait_recv()
         bz = me.at(0, IN_GROUPS[g])[1]
 
         @pl.loop(0, X * Q // U)
@@ -228,53 +246,63 @@
             forward_line(g - 1)
     assert not coming
 
-    @pl.loop(0, NBLK // 2)
-    def _(i):
-        for u in range(2):
-            b = i * 2 + u
-            v = pre[meta[LAST_, b]].reshape(T, BS)
-            s = jax.nn.sigmoid(v)
-            slope = s * (1.0 + v * (1.0 - s))
-            ag[b] = (ogb[meta[COLS_, b]].astype(F32) * slope).astype(BF16)
-
-    to_other = pltpu.make_async_remote_copy(
-        src_ref=ig_out, dst_ref=rec_ref, send_sem=send_ig, recv_sem=recv_ig,
-        device_id=me.other_section, device_id_type=MESH)
-
-    def input_grad(first, n):
+    def slopes(g):
+        bz = me.at(0, OUT_GROUPS[g])[1]
+
+        @pl.loop(0, X * Q // 4)
+        def _(bx):
+            for u in range(4):
+                b = (bx * Z + bz) * Q + u
+                v = pre[meta[LAST_, b]].reshape(T, BS)
+                s = jax.nn.sigmoid(v)
+                slope = s * (1.0 + v * (1.0 - s))
+                grad = (ogb[meta[COLS_, b]].astype(F32) * slope).astype(BF16)
+                ag[b] = grad.reshape(micro, tok, BS)
+
+    half = micro // 2
+    to_other = [pltpu.make_async_remote_copy(
+        src_ref=ig_out.at[pl.ds(h * half, half)], dst_ref=rec_ref.at[pl.ds(h * half, half)],
+        send_sem=send_ig.at[h], recv_sem=recv_ig.at[h],
+        device_id=me.other_section, device_id_type=MESH) for h in range(2)]
+
+    def input_grad(h, blocks, first):
+        mine_at = range(h * half, (h + 1) * half)
+
         @pl.when(me.section == 1)
         def _():
-            @pl.loop(first // U, (first + n) // U)
+            @pl.loop(first // U, (first + blocks) // U)
             def _(i):
                 prods = []
                 for u in range(U):
                     b = i * U + u
                     weight = w[b // (Z * Q), (b // Q) % Z, pl.ds(pl.multiple_of((b % Q) * BS, BS), BS), :]
+                    grad = jnp.concatenate([ag[b, order[k]] for k in mine_at], axis=0)
                     prods.append(lax.dot_general(
-                        ag[b], weight, (((1,), (1,)), ((), ())), preferred_element_type=F32))
+                        grad, weight, (((1,), (1,)), ((), ())), preferred_element_type=F32))
                 for u in range(U):
                     b = i * U + u
-                    pre[b] = prods[u].reshape(micro, tok, BS) + pre[meta[ROW_PREV_, b]]
-
-    def send_input_grad():
+                    for n, k in enumerate(mine_at):
+                        pre[b, k] = prods[u][n * tok:(n + 1) * tok] + pre[meta[ROW_PREV_, b], k]
+
+    def send_input_grad(h):
         @pl.when(me.section == 1)
         def _():
             @pl.loop(0, n_rows)
             def _(r):
                 end = meta[ROW_END_, r]
-                for i in range(micro):
-                    ig_out[i, :, lanes(r)] = pre[end, order[i]].astype(BF16)
-
-            to_other.start()
-
-            @pl.loop(0, micro)
+                for k in range(h * half, (h + 1) * half):
+                    ig_out[k, :, lanes(r)] = pre[end, k].astype(BF16)
+
+            to_other[h].start()
+
+            @pl.loop(h * half, (h + 1) * half)
             def _(i):
                 rec_ref[i] = jnp.zeros(rec_ref.shape[1:], BF16)
 
     def product(dx, dz, q):
         bx, bz = me.at(dx, dz)
         b = (bx * Z + bz) * Q + q
-        return jnp.dot(xt[meta[ROWS_, b]], ag[b], preferred_element_type=F32)
+        return jnp.dot(xt[meta[ROWS_, b]], ag[b].reshape(T, BS), preferred_element_type=F32)
 
     halved = []
 
@@ -336,19 +364,22 @@
                 mine[A_ROWS:PAIR, :] = total
 
     n = len(OUT_GROUPS)
-    for g in range(n + 5):
-        if g < n:
-            share(g)
-        if 2 <= g < n + 2:
-            own(g - 2)
-        if g < 4:
-            input_grad(g * (NBLK // 4), NBLK // 4)
-        if g == 4:
-            send_input_grad()
-        if g == n + 4:
+    for g in range(n):
+        slopes(g)
+        share(g)
+        if g >= 5:
+            own(g - 5)
+    input_grad(0, NBLK, 0)
+    send_input_grad(0)
+    own(3)
+    for i in range(4):
+        input_grad(1, NBLK // 4, i * (NBLK // 4))
+        own(4 + i)
+    send_input_grad(1)
+    for g in range(n):
+        if g == n - 1:
             second_b()
-        if g >= 5:
-            second_a(g - 5)
+        second_a(g)
 
     total_a, total_b = mine[0:A_ROWS, :], mine[A_ROWS:PAIR, :]
     for g, dz in enumerate(OUT_GROUPS):
@@ -368,11 +399,13 @@
 
     @pl.when(me.section == 1)
     def _():
-        to_other.wait_send()
+        for c in to_other:
+            c.wait_send()
 
     @pl.when(me.section == 0)
     def _():
-        to_other.wait_recv()
+        for c in to_other:
+            c.wait_recv()
 
 
 def gradients(pat, order, blocks, x, og):
@@ -400,7 +433,7 @@
             V(x.shape, BF16), V(og.shape, BF16),
             V((n_rows, T, BS), BF16), V((n_rows, BS, T), BF16), V((n_cols, T, BS), BF16),
             V((NBLK + 1, micro, tok, BS), F32),
-            V((NBLK, T, BS), BF16),
+            V((NBLK, micro, tok, BS), BF16),
             V(x.shape, BF16),
             V((n, X, PAIR, BS), BF16), V((n, X, PAIR, BS), BF16),
             V((X - 1, n, A_ROWS, BS), BF16), V((X - 1, n, A_ROWS, BS), BF16),
@@ -409,12 +442,12 @@
             V((X, B_ROWS, BS), F32), V((X, B_ROWS, BS), BF16), V((X, B_ROWS, BS), BF16),
             V((PAIR, BS), F32), V((2, PAIR, BS), BF16),
             pltpu.SemaphoreType.DMA((N_COPIES,)), pltpu.SemaphoreType.DMA((N_COPIES,)),
-            pltpu.SemaphoreType.DMA, pltpu.SemaphoreType.DMA, pltpu.SemaphoreType.DMA((6,)),
+            pltpu.SemaphoreType.DMA((2,)), pltpu.SemaphoreType.DMA((2,)), pltpu.SemaphoreType.DMA((6,)),
         ],
         compiler_params=pltpu.CompilerParams(
             collective_id=0, has_side_effects=True, vmem_limit_bytes=52 * 2**20),
         name="gradients",
-    )(pat, order, blocks, x, og)
+    )(*(pltpu.with_memory_space_constraint(v, pltpu.HBM) for v in (pat, order, blocks, x, og)))
 
 
 def deliver_kernel(a_in, b_in, a_out, b_out, sem):

time: 77.8 us -> 71.2 us (0.915)
  Pallas kernels: 74.7 us -> 70.5 us
  local copies, waits for them, and re-layouts: 2.23 us -> 0 us
    pallas_call x1, Pallas kernels: 73.7 us -> 69.5 us  [gradients(): pl.pallas_call(kernel, out_shape=(jax.ShapeDtypeStruct(x.shape, BF16), ja...]
    unnamed x6 -> x0, local copies, waits for them, and re-layouts: 2.23 us -> none
where the time goes in v4:
time: 71.2 us; the launch traced here: 71.1 us
  Pallas kernels  70.5 us (99%)
    pallas_call x1, Pallas kernels, gradients(): pl.pallas_call(kernel, out_shape=(jax.ShapeDtypeStruct(x.shape, BF16), ja...  69.5 us

profile of v4, /device:TPU:9, one launch (start us, length us, event | category | flops | bytes accessed | tf_op | source)
XLA Modules:
  0.0 71.1 jit_solution(6989944679494058927)
XLA Ops:
  0.6 69.5 %gradients.1 = (bf16[4,32,3584]{2,1,0:T(8,128)(2,1)S(1)}, f32[512,128]{1,0:T(8,128)S(1)}) custom-call(s32[2,4]{1,0:T(2,128)} %bitcast.11, s32[4]{0:T(128)} %order_hbm.1, bf16[512,128]{1,0:T(8,128)(2,1)} %bitcast.10, bf16[4,32,3584]{2,1,0:T(8,128)(2,1)} %bitcast.9, bf16[4,32,14336]{2,1,0:T(8,128)(2,1)} %bitcast.8), custom_call_target="tpu_custom_call" | custom-call | tf_op jit(solution)/shard_map/gradients/pallas_call | solution.py:419
  70.1 1.0 %deliver.1 = (bf16[4,32,3584]{2,1,0:T(8,128)(2,1)}, f32[512,128]{1,0:T(8,128)}) custom-call(bf16[4,32,3584]{2,1,0:T(8,128)(2,1)S(1)} %get-tuple-element.6.a_in, f32[512,128]{1,0:T(8,128)S(1)} %get-tuple-element.7.b_in), custom_call_target="tpu_custom_call" | custom-call | tf_op jit(solution)/shard_map/deliver/pallas_call | solution.py:463

commit v5 on v4

--- a/solution.py
+++ b/solution.py
@@ -22,7 +22,8 @@
 LATE = 6
 OUT_GROUPS = (4, 3, -3, 2, -2, 1, -1, 0)
 ROWS_, COLS_, PREV_, LAST_, ROW_PREV_, ROW_END_ = range(6)
-N_COPIES = 7 + 3 + 62 + 14 + 8 + 24 + 7 + 7 + 3 + 2
+PIECES = 2
+N_COPIES = 7 + 3 + 62 + 14 + 8 + 24 + 7 + 7 + 3 + 2 * (1 + PIECES)
 
 
 class Place:
@@ -61,6 +62,7 @@
     def finish(self):
         for copy in self.made:
             copy.wait_send()
+        self.made = []
 
 
 def announce(devices):
@@ -376,25 +378,46 @@
         input_grad(1, NBLK // 4, i * (NBLK // 4))
         own(4 + i)
     send_input_grad(1)
+    scale = 1.0 / 128.0
+    crossing, last = [], []
+
+    def to_twin(at, total):
+        halves[0, at, :] = total.astype(BF16)
+        crossing.append((at, copies.start(halves.at[0, at], halves.at[1, at], me.twin)))
+
+    def to_sibling():
+        at, copy = crossing.pop(0)
+        copy.wait_recv()
+        rows = pl.ds(first_row + at.start, at.size)
+        wg_ref[rows, :] = (halves[0, at, :].astype(F32) + halves[1, at, :].astype(F32)) * scale
+        last.append(copies.start(wg_ref.at[rows], wg_ref.at[rows], me.sibling))
+
     for g in range(n):
+        if g == 3:
+            second_b()
         if g == n - 1:
-            second_b()
+            total = mine[A_ROWS:PAIR, :]
+            for dx in range(1, X):
+                sent["b2", dx].wait_recv()
+                total += rb2[dx].astype(F32)
+            to_twin(pl.ds(A_ROWS, B_ROWS), total)
         second_a(g)
 
-    total_a, total_b = mine[0:A_ROWS, :], mine[A_ROWS:PAIR, :]
     for g, dz in enumerate(OUT_GROUPS):
         if dz != 0:
             sent["a2", g].wait_recv()
-            total_a += ra2[g].astype(F32)
-    for dx in range(1, X):
-        sent["b2", dx].wait_recv()
-        total_b += rb2[dx].astype(F32)
-    halves[0, 0:A_ROWS, :] = total_a.astype(BF16)
-    halves[0, A_ROWS:PAIR, :] = total_b.astype(BF16)
-    copies.start(halves.at[0], halves.at[1], me.twin).wait_recv()
-    scale = 1.0 / 128.0
-    wg_ref[pair_rows, :] = (halves[0].astype(F32) + halves[1].astype(F32)) * scale
-    copies.start(wg_ref.at[pair_rows], wg_ref.at[pair_rows], me.sibling).wait_recv()
+    for i in range(PIECES):
+        at = pl.ds(i * (A_ROWS // PIECES), A_ROWS // PIECES)
+        total = mine[at, :]
+        for g, dz in enumerate(OUT_GROUPS):
+            if dz != 0:
+                total += ra2[g, at, :].astype(F32)
+        to_twin(at, total)
+    copies.finish()
+    while crossing:
+        to_sibling()
+    for c in last:
+        c.wait_recv()
     copies.finish()
 
     @pl.when(me.section == 1)

time: 71.2 us -> 71 us (level)
  no operation moved by 1% of the time
where the time goes in v5:
time: 71 us; the launch traced here: 70.9 us
  Pallas kernels  70.2 us (99%)
    pallas_call x1, Pallas kernels, gradients(): pl.pallas_call(kernel, out_shape=(jax.ShapeDtypeStruct(x.shape, BF16), ja...  69.2 us

profile of v5, /device:TPU:9, one launch (start us, length us, event | category | flops | bytes accessed | tf_op | source)
XLA Modules:
  0.0 70.9 jit_solution(9428761550264334661)
XLA Ops:
  0.6 69.2 %gradients.1 = (bf16[4,32,3584]{2,1,0:T(8,128)(2,1)S(1)}, f32[512,128]{1,0:T(8,128)S(1)}) custom-call(s32[2,4]{1,0:T(2,128)} %bitcast.11, s32[4]{0:T(128)} %order_hbm.1, bf16[512,128]{1,0:T(8,128)(2,1)} %bitcast.10, bf16[4,32,3584]{2,1,0:T(8,128)(2,1)} %bitcast.9, bf16[4,32,14336]{2,1,0:T(8,128)(2,1)} %bitcast.8), custom_call_target="tpu_custom_call" | custom-call | tf_op jit(solution)/shard_map/gradients/pallas_call | solution.py:442
  69.8 1.0 %deliver.1 = (bf16[4,32,3584]{2,1,0:T(8,128)(2,1)}, f32[512,128]{1,0:T(8,128)}) custom-call(bf16[4,32,3584]{2,1,0:T(8,128)(2,1)S(1)} %get-tuple-element.6.a_in, f32[512,128]{1,0:T(8,128)S(1)} %get-tuple-element.7.b_in), custom_call_target="tpu_custom_call" | custom-call | tf_op jit(solution)/shard_map/deliver/pallas_call | solution.py:486

commit v6 on v5

--- a/solution.py
+++ b/solution.py
@@ -22,6 +22,7 @@
 LATE = 6
 OUT_GROUPS = (4, 3, -3, 2, -2, 1, -1, 0)
 ROWS_, COLS_, PREV_, LAST_, ROW_PREV_, ROW_END_ = range(6)
+LEAD = 5
 PIECES = 2
 N_COPIES = 7 + 3 + 62 + 14 + 8 + 24 + 7 + 7 + 3 + 2 * (1 + PIECES)
 
@@ -368,13 +369,19 @@
     n = len(OUT_GROUPS)
     for g in range(n):
         slopes(g)
-        share(g)
-        if g >= 5:
-            own(g - 5)
+        if g < 4:
+            share(g)
+        if g >= LEAD:
+            own(g - LEAD)
     input_grad(0, NBLK, 0)
     send_input_grad(0)
-    own(3)
+    share(4)
+    share(5)
+    for g in range(n - LEAD, 4):
+        own(g)
     for i in range(4):
+        if i < 2:
+            share(6 + i)
         input_grad(1, NBLK // 4, i * (NBLK // 4))
         own(4 + i)
     send_input_grad(1)

time: 71 us -> 70.1 us (0.987)
  Pallas kernels: 70.2 us -> 69.3 us
    pallas_call x1, Pallas kernels: 69.2 us -> 68.3 us  [gradients(): pl.pallas_call(kernel, out_shape=(jax.ShapeDtypeStruct(x.shape, BF16), ja...]
where the time goes in v6:
time: 70.1 us; the launch traced here: 70 us
  Pallas kernels  69.3 us (99%)
    pallas_call x1, Pallas kernels, gradients(): pl.pallas_call(kernel, out_shape=(jax.ShapeDtypeStruct(x.shape, BF16), ja...  68.3 us

profile of v6, /device:TPU:9, one launch (start us, length us, event | category | flops | bytes accessed | tf_op | source)
XLA Modules:
  0.0 70.0 jit_solution(7614454262525967183)
XLA Ops:
  0.6 68.3 %gradients.1 = (bf16[4,32,3584]{2,1,0:T(8,128)(2,1)S(1)}, f32[512,128]{1,0:T(8,128)S(1)}) custom-call(s32[2,4]{1,0:T(2,128)} %bitcast.11, s32[4]{0:T(128)} %order_hbm.1, bf16[512,128]{1,0:T(8,128)(2,1)} %bitcast.10, bf16[4,32,3584]{2,1,0:T(8,128)(2,1)} %bitcast.9, bf16[4,32,14336]{2,1,0:T(8,128)(2,1)} %bitcast.8), custom_call_target="tpu_custom_call" | custom-call | tf_op jit(solution)/shard_map/gradients/pallas_call | solution.py:449
  69.0 1.0 %deliver.1 = (bf16[4,32,3584]{2,1,0:T(8,128)(2,1)}, f32[512,128]{1,0:T(8,128)}) custom-call(bf16[4,32,3584]{2,1,0:T(8,128)(2,1)S(1)} %get-tuple-element.6.a_in, f32[512,128]{1,0:T(8,128)S(1)} %get-tuple-element.7.b_in), custom_call_target="tpu_custom_call" | custom-call | tf_op jit(solution)/shard_map/deliver/pallas_call | solution.py:493

commit v7 on v6

--- a/solution.py
+++ b/solution.py
@@ -22,7 +22,7 @@
 LATE = 6
 OUT_GROUPS = (4, 3, -3, 2, -2, 1, -1, 0)
 ROWS_, COLS_, PREV_, LAST_, ROW_PREV_, ROW_END_ = range(6)
-LEAD = 5
+LEAD = 6
 PIECES = 2
 N_COPIES = 7 + 3 + 62 + 14 + 8 + 24 + 7 + 7 + 3 + 2 * (1 + PIECES)
 

time: 70.1 us -> 70.6 us (level)
  no operation moved by 1% of the time
where the time goes in v7:
time: 70.6 us; the launch traced here: 70.5 us
  Pallas kernels  69.9 us (99%)
    pallas_call x1, Pallas kernels, gradients(): pl.pallas_call(kernel, out_shape=(jax.ShapeDtypeStruct(x.shape, BF16), ja...  68.8 us

profile of v7, /device:TPU:9, one launch (start us, length us, event | category | flops | bytes accessed | tf_op | source)
XLA Modules:
  0.0 70.5 jit_solution(6162787015852634291)
XLA Ops:
  0.6 68.8 %gradients.1 = (bf16[4,32,3584]{2,1,0:T(8,128)(2,1)S(1)}, f32[512,128]{1,0:T(8,128)S(1)}) custom-call(s32[2,4]{1,0:T(2,128)} %bitcast.11, s32[4]{0:T(128)} %order_hbm.1, bf16[512,128]{1,0:T(8,128)(2,1)} %bitcast.10, bf16[4,32,3584]{2,1,0:T(8,128)(2,1)} %bitcast.9, bf16[4,32,14336]{2,1,0:T(8,128)(2,1)} %bitcast.8), custom_call_target="tpu_custom_call" | custom-call | tf_op jit(solution)/shard_map/gradients/pallas_call | solution.py:449
  69.5 1.0 %deliver.1 = (bf16[4,32,3584]{2,1,0:T(8,128)(2,1)}, f32[512,128]{1,0:T(8,128)}) custom-call(bf16[4,32,3584]{2,1,0:T(8,128)(2,1)S(1)} %get-tuple-element.6.a_in, f32[512,128]{1,0:T(8,128)S(1)} %get-tuple-element.7.b_in), custom_call_target="tpu_custom_call" | custom-call | tf_op jit(solution)/shard_map/deliver/pallas_call | solution.py:493
